TPU v7x, 512 devices: a whole 4x8x8 slice. The times are simulated.
512 devices in a mesh: row: 64 (over z, y), rep: 8 (over x, core).
Axes of the slice: x: 4, y: 8, z: 8, core: 2. Of those that a mesh axis runs over, the one named last changes fastest.
Arguments:
- features: bfloat16 [32768, 128], P('row'), may hold values from -6 to 6
- edge_tiles: bfloat16 [8192, 128, 128], P(('row', 'rep')), may hold values from -0.09375 to 0.09375
- tile_owner: int32 [8192, 1], P(('row', 'rep')), may hold values from 0 to 63; in each aligned block of 16 rows (0 to 15, 16 to 31, ...) at most 2 rows name the same one
- tile_block: int32 [8192], P(('row', 'rep')), may hold values from 0 to 3
- tile_row: int32 [8192], P(('row', 'rep')), may hold values from 0 to 3
- w_self: bfloat16 [128, 256], replicated, may hold values from -0.5 to 0.5
- w_neigh: bfloat16 [128, 256], replicated, may hold values from -0.5 to 0.5
- bias_vector: float32 [256], replicated, may hold values from -3 to 3
- cotangent: bfloat16 [32768, 256], P(('row', 'rep')), may hold values from -6 to 6
Outputs:
- hidden: bfloat16 [32768, 256], P(('row', 'rep'))
- grad_features: float32 [32768, 128], P(('row', 'rep'))
- grad_self: float32 [128, 256], replicated
- grad_neigh: float32 [128, 256], replicated
- grad_bias: float32 [256], replicated
Inputs may be any that keep to these rules, and one draw needn't show every extreme that they name: `tile_owner`: among the 16 tiles of one device, no value occurs more than 2 times, and some value occurs exactly 2 times.
All inputs are finite; a program needn't handle non-finite values.
Results may differ from a plain program's by a relative error of at most 0.014.
Values may be sent and summed in bfloat16 or wider, within the bound.
A program may use at most 64 MiB of HBM per device.

v0:
```python
import jax
import jax.numpy as jnp
from jax import lax
from jax.sharding import PartitionSpec as P


def per_device(
    features, edge_tiles, tile_owner, tile_block, tile_row, w_self, w_neigh, bias_vector, cotangent
):
    row_count = lax.axis_size("row")
    rep_count = lax.axis_size("rep")
    tile_count = edge_tiles.shape[0]
    block_size = edge_tiles.shape[1]
    width = features.shape[1]
    node_count = features.shape[0]
    block_count = node_count // block_size
    share_rows = node_count // rep_count
    capacity = max(2, (2 * tile_count + row_count - 1) // row_count)
    highest = lax.Precision.HIGHEST
    owners = tile_owner[:, 0]
    positions = jnp.arange(tile_count, dtype=jnp.int32)
    same_owner = (owners[:, None] == owners[None, :]) & (positions[:, None] > positions[None, :])
    slot_of = jnp.sum(same_owner.astype(jnp.int32), axis=1)
    flat_slot = owners * capacity + slot_of
    request = jnp.full((row_count * capacity,), -1, jnp.int32).at[flat_slot].set(tile_block)
    request = request.reshape(row_count, capacity)
    incoming = lax.all_to_all(request, "row", split_axis=0, concat_axis=0, tiled=True)
    gathered = lax.all_gather(features, "row", axis=0, tiled=True)
    all_blocks = gathered.reshape(row_count * block_count, block_size, width)
    fetched = jnp.take(all_blocks, owners * block_count + tile_block, axis=0)
    products = jnp.einsum("tij,tjf->tif", edge_tiles, fetched, preferred_element_type=jnp.float32)
    row_onehot = (tile_row[:, None] == jnp.arange(block_count, dtype=jnp.int32)[None, :]).astype(
        jnp.float32
    )
    partial_value = jnp.einsum("tn,tif->nif", row_onehot, products, precision=highest).reshape(
        node_count, width
    )
    rep_index = lax.axis_index("rep")
    total = lax.psum(partial_value, "rep")
    own_sum = lax.dynamic_slice_in_dim(total, rep_index * share_rows, share_rows, 0)
    aggregate_b = own_sum.astype(jnp.bfloat16)
    own_rows = lax.dynamic_slice_in_dim(features, rep_index * share_rows, share_rows, 0)
    preact = (
        jnp.dot(own_rows, w_self, preferred_element_type=jnp.float32)
        + jnp.dot(aggregate_b, w_neigh, preferred_element_type=jnp.float32)
        + bias_vector
    )
    hidden = jax.nn.silu(preact).astype(jnp.bfloat16)
    sigmoid_part = jax.nn.sigmoid(preact)
    dpre = cotangent.astype(jnp.float32) * sigmoid_part * (1.0 + preact * (1.0 - sigmoid_part))
    dpre_b = dpre.astype(jnp.bfloat16)
    contract_rows = (((0,), (0,)), ((), ()))
    local_self = lax.dot_general(
        own_rows, dpre_b, contract_rows, preferred_element_type=jnp.float32
    )
    local_neigh = lax.dot_general(
        aggregate_b, dpre_b, contract_rows, preferred_element_type=jnp.float32
    )
    local_bias = jnp.sum(dpre, axis=0)
    summed_self, summed_neigh, summed_bias = lax.psum(
        (local_self, local_neigh, local_bias), ("row", "rep")
    )
    scale = float(node_count * row_count) ** (-0.5)
    contract_cols = (((1,), (1,)), ((), ()))
    dagg = lax.dot_general(
        dpre_b, w_neigh, contract_cols, preferred_element_type=jnp.float32
    ).astype(jnp.bfloat16)
    block_dagg = lax.all_gather(dagg, "rep", axis=0, tiled=True).reshape(
        block_count, block_size, width
    )
    rows_for_tiles = jnp.take(block_dagg, tile_row, axis=0)
    transposed = jnp.einsum(
        "tij,tif->tjf", edge_tiles, rows_for_tiles, preferred_element_type=jnp.float32
    ).astype(jnp.bfloat16)
    outgoing = (
        jnp.zeros((row_count * capacity, block_size, width), jnp.bfloat16)
        .at[flat_slot]
        .set(transposed)
    )
    returned = lax.all_to_all(
        outgoing.reshape(row_count, capacity, block_size, width),
        "row",
        split_axis=0,
        concat_axis=0,
        tiled=True,
    )
    block_onehot = (
        incoming.reshape(-1)[:, None] == jnp.arange(block_count, dtype=jnp.int32)[None, :]
    ).astype(jnp.bfloat16)
    back_partial = jnp.einsum(
        "sn,sif->nif",
        block_onehot,
        returned.reshape(row_count * capacity, block_size, width),
        preferred_element_type=jnp.float32,
    ).reshape(node_count, width)
    back_share = lax.psum_scatter(
        back_partial.astype(jnp.bfloat16), "rep", scatter_dimension=0, tiled=True
    ).astype(jnp.float32)
    grad_features = (
        lax.dot_general(dpre_b, w_self, contract_cols, preferred_element_type=jnp.float32)
        + back_share
    )
    return (hidden, grad_features, summed_self * scale, summed_neigh * scale, summed_bias * scale)


def solution(mesh):
    in_specs = (
        P("row", None),
        P(("row", "rep"), None, None),
        P(("row", "rep"), None),
        P(("row", "rep")),
        P(("row", "rep")),
        P(),
        P(),
        P(),
        P(("row", "rep"), None),
    )
    out_specs = (P(("row", "rep"), None), P(("row", "rep"), None), P(), P(), P())
    return jax.shard_map(
        per_device, mesh=mesh, in_specs=in_specs, out_specs=out_specs, check_vma=False
    )
```

profile of v0, /device:TPU:1, one launch (start us, length us, event | category | flops | bytes accessed | tf_op | source)
XLA Modules:
  0.0 585.1 jit_solution(11094190233930706452)
XLA Ops:
  8.0 0.9 convert_reduce_fusion
  9.5 0.8 scatter_custom_fusion
  10.3 0.8 all_to_all.9
  11.0 17.1 %all-to-all-start = ((s32[64,1,2]{2,1,0:T(1,128)}), s32[64,1,2]{2,1,0:T(1,128)S(1)}, u32[]{:S(2)}, u32[]{:S(2)}) async-start(s32[64,1,2]{2,1,0:T(1,128)} %bitcast.7), calls=%async_computation | async-start | bytes 65536 | tf_op jit(solution)/shard_map/all_to_all | solution.py:27
  28.2 0.7 compare_and_fusion.1
  30.2 1.0 fusion.10
  31.2 84.8 %all-gather.2.cloned.1.call-done = bf16[32768,128]{1,0:T(8,128)(2,1)} async-done(((bf16[512,128]{1,0:T(8,128)(2,1)}), bf16[32768,128]{1,0:T(8,128)(2,1)}) %all-gather.2.cloned.1.call-update) | async-done | bytes 8388624 | tf_op jit(solution)/shard_map/all_gather | solution.py:28
  116.0 4.0 gather_fusion
  121.7 25.4 %all-reduce.5 = bf16[512,128]{1,0:T(8,128)(2,1)S(1)} all-reduce(f32[512,128]{1,0:T(8,128)S(1)} %bitcast.41), channel_id=1, replica_groups=mesh['row'=64,'rep'=8] {'rep'}, use_global_device_ids=true, to_apply=%region_0.0 | all-reduce | flops 65536 | bytes 393216 | tf_op jit(solution)/shard_map/psum | solution.py:39
  147.1 0.8 fusion.30
  148.1 16.3 %all_gather.7 = bf16[512,128]{1,0:T(8,128)(2,1)S(1)} all-gather(bf16[64,128]{1,0:T(8,128)(2,1)S(1)} %convolution_convert_fusion.2), channel_id=1, replica_groups=mesh['row'=64,'rep'=8] {'rep'}, dimensions={0}, use_global_device_ids=true | all-gather | bytes 147456 | tf_op jit(solution)/shard_map/all_gather | solution.py:68
  165.7 3.0 broadcast_in_dim.40
  168.7 2.6 scatter_fusion
  171.3 8.5 %copy.37 = bf16[64,2,128,128]{3,1,2,0:T(2,128)(2,1)} copy(bf16[64,2,128,128]{3,2,1,0:T(8,128)(2,1)} %bitcast.38) | data formatting | bytes 8388608 | tf_op jit(solution)/shard_map/reshape | solution.py:81
  179.8 10.0 %all-to-all-start.1 = ((bf16[64,2,128,128]{3,1,2,0:T(2,128)(2,1)}), bf16[64,2,128,128]{3,1,2,0:T(2,128)(2,1)}, u32[]{:S(2)}, u32[]{:S(2)}) async-start(bf16[64,2,128,128]{3,1,2,0:T(2,128)(2,1)} %copy.37), calls=%async_computation.1 | async-start | bytes 8388608 | tf_op jit(solution)/shard_map/all_to_all | solution.py:80
  190.4 0.7 reduce.3
  191.3 0.9 fusion.13
  192.1 1.6 fusion.8
  193.8 223.6 %psum.31 = f32[256]{0:T(256)S(1)} all-reduce(f32[256]{0:T(256)S(1)} %get-tuple-element.7), channel_id=1, replica_groups=mesh['row'=64,'rep'=8] {'row','rep'}, use_global_device_ids=true, to_apply=%region_8.9 | all-reduce | flops 256 | bytes 2048 | tf_op jit(solution)/shard_map/psum | solution.py:60
  417.4 6.9 %copy.38 = bf16[64,2,128,128]{3,1,0,2:T(2,128)(2,1)S(1)} copy(bf16[64,2,128,128]{3,1,2,0:T(2,128)(2,1)} %all-to-all-done.1) | data formatting | bytes 8388608 | tf_op jit(solution)/shard_map/all_to_all | solution.py:80
  426.2 117.5 %all-reduce.4.cloned.1.call-done = (f32[128,256]{1,0:T(8,128)}, f32[128,256]{1,0:T(8,128)}) async-done(((f32[128,256]{1,0:T(8,128)}, f32[128,256]{1,0:T(8,128)}), (f32[128,256]{1,0:T(8,128)}, f32[128,256]{1,0:T(8,128)})) %all-reduce.4.cloned.1.call-update) | async-done | bytes 262160 | tf_op jit(solution)/shard_map/psum | solution.py:60
  543.8 1.7 broadcast_multiply_fusion
  545.4 31.7 %reduce-scatter.2.cloned.1.call-done = bf16[64,128]{1,0:T(8,128)(2,1)} async-done(((bf16[512,128]{1,0:T(8,128)(2,1)}), bf16[64,128]{1,0:T(8,128)(2,1)}) %reduce-scatter.2.cloned.1.call-update) | async-done | bytes 16400 | tf_op jit(solution)/shard_map/reduce_scatter | solution.py:96
  577.1 1.5 convolution_add_fusion.1
  (38 shorter events, 8.5 us)
Async XLA Ops:
  7.2 112.9 %copy-start = (bf16[16,128,128]{2,1,0:T(8,128)(2,1)S(1)}, bf16[16,128,128]{2,1,0:T(8,128)(2,1)}, u32[]{:S(2)}) copy-start(bf16[16,128,128]{2,1,0:T(8,128)(2,1)} %param.10) | copy-start | bytes 1572868
  7.2 114.1 %copy-start.3 = (s32[16]{0:T(128)S(1)}, s32[16]{0:T(128)}, u32[]{:S(2)}) copy-start(s32[16]{0:T(128)} %param.13) | copy-start | bytes 196
  7.2 139.9 %copy-start.2 = (bf16[128,256]{1,0:T(8,128)(2,1)S(1)}, bf16[128,256]{1,0:T(8,128)(2,1)}, u32[]{:S(2)}) copy-start(bf16[128,256]{1,0:T(8,128)(2,1)} %param.15) | copy-start | bytes 196612
  7.2 139.9 %copy-start.5 = (f32[256]{0:T(256)S(1)}, f32[256]{0:T(256)}, u32[]{:S(2)}) copy-start(f32[256]{0:T(256)} %param.16) | copy-start | bytes 3076
  7.2 139.9 %copy-start.4 = (bf16[64,256]{1,0:T(8,128)(2,1)S(1)}, bf16[64,256]{1,0:T(8,128)(2,1)}, u32[]{:S(2)}) copy-start(bf16[64,256]{1,0:T(8,128)(2,1)} %param.17) | copy-start | bytes 98308
  7.2 108.8 %all-gather.2.cloned.1.call-start = ((), (), s32[]{:S(2)}) async-start(), calls=%async_computation.3 | async-start | bytes 8519680 | tf_op jit(solution)/shard_map/all_gather | solution.py:28
  11.0 168.7 %all-to-all-start = ((s32[64,1,2]{2,1,0:T(1,128)}), s32[64,1,2]{2,1,0:T(1,128)S(1)}, u32[]{:S(2)}, u32[]{:S(2)}) async-start(s32[64,1,2]{2,1,0:T(1,128)} %bitcast.7), calls=%async_computation | async-start | bytes 65536 | tf_op jit(solution)/shard_map/all_to_all | solution.py:27
  179.8 237.6 %all-to-all-start.1 = ((bf16[64,2,128,128]{3,1,2,0:T(2,128)(2,1)}), bf16[64,2,128,128]{3,1,2,0:T(2,128)(2,1)}, u32[]{:S(2)}, u32[]{:S(2)}) async-start(bf16[64,2,128,128]{3,1,2,0:T(2,128)(2,1)} %copy.37), calls=%async_computation.1 | async-start | bytes 8388608 | tf_op jit(solution)/shard_map/all_to_all | solution.py:80
  189.8 353.9 %all-reduce.4.cloned.1.call-start = ((), (), s32[]{:S(2)}) async-start(), calls=%async_computation.5 | async-start | bytes 524288 | tf_op jit(solution)/shard_map/psum | solution.py:60
  193.7 383.4 %reduce-scatter.2.cloned.1.call-start = ((), (), s32[]{:S(2)}) async-start(), calls=%async_computation.4 | async-start | bytes 147456 | tf_op jit(solution)/shard_map/reduce_scatter | solution.py:96
  424.3 152.8 %copy-start.1 = (bf16[128,256]{1,0:T(8,128)(2,1)S(1)}, bf16[128,256]{1,0:T(8,128)(2,1)}, u32[]{:S(2)}) copy-start(bf16[128,256]{1,0:T(8,128)(2,1)} %param.14) | copy-start | bytes 196612
Sparse Core Ops, SparseCore 0:
  11.1 104.8 all-gather.1
  196.4 347.2 all-reduce.3
  546.8 30.3 reduce-scatter.1
where the time goes:
time: 588 us; the launch traced here: 585 us
  blocking collectives  265 us (45%)
  waiting for transfers between devices  235 us (40%)
  local copies, waits for them, and re-layouts  29.3 us (5%)
  starting transfers between devices  27.3 us (5%)
  between operations  14 us (2%)
  matrix products  8.03 us (1%)
  other arithmetic  6.57 us (1%)
    psum x1, blocking collectives, per_device(): lax.psum((local_self, local_neigh, local_bias), ('row', 'rep'))  224 us
    psum x1, waiting for transfers between devices, per_device(): lax.psum((local_self, local_neigh, local_bias), ('row', 'rep'))  118 us
    all_gather x1, waiting for transfers between devices, per_device(): gathered = lax.all_gather(features, 'row', axis=0, tiled=True)  84.8 us
    reduce_scatter x1, waiting for transfers between devices, per_device(): lax.psum_scatter(back_partial.astype(jnp.bfloat16), 'rep', scatter_dimens...  31.7 us
    psum x1, blocking collectives, per_device(): total = lax.psum(partial_value, 'rep')  25.4 us
    all_to_all x1, starting transfers between devices, per_device(): lax.all_to_all(request, 'row', split_axis=0, concat_axis=0, tiled=True)  17.1 us
    all_gather x1, blocking collectives, per_device(): lax.all_gather(dagg, 'rep', axis=0, tiled=True)  16.3 us
  transfers between devices with their start and end apart: 5, of which 3 were waited for; matrix products, arithmetic and copies ran while one was open for 7% of the time, Pallas kernels for 0%

commit v1 on v0

v1 whole, which is shorter than its diff:
```python
import jax
import jax.numpy as jnp
from jax import lax
from jax.experimental import pallas as pl
from jax.experimental.pallas import tpu as pltpu
from jax.sharding import PartitionSpec as P

MESH = pl.DeviceIdType.MESH
BF = jnp.bfloat16
F32 = jnp.float32


def swap_matrix(first, second):
    size = first * second
    out = lax.broadcasted_iota(jnp.int32, (size, size), 0)
    src = lax.broadcasted_iota(jnp.int32, (size, size), 1)
    match = (out // first == src % second) & (out % first == src // second)
    return match.astype(F32).astype(BF)


def dot(a, b):
    return jnp.dot(a, b, preferred_element_type=F32)


def make_kernel(nz, ny, nrep, tpd, blk, width, hid, nbd):
    cs = blk // nrep
    nodes = nbd * blk
    share = nodes // nrep
    half = nbd // 2
    npos = nbd * nz * ny
    hpos = npos // 2
    tiles_all = nrep * tpd
    scale = float(nz * ny * nodes) ** -0.5
    assert nz == ny and hid == 2 * width
    wrows = 4 * width // nrep
    yrows = wrows // ny

    def kernel(
        feat, tiles, owner, tblock, trow, w_self, w_neigh, bias, cot,
        hid_o, gf_o, gs_o, gn_o, gb_o,
        meta_s, meta, xt, ysend, tt, f1, f2, ttm, fg, a0, a1, dense, dg0, dg, o0, b1, b2s, b2,
        r0, r1, gl, g1, g2s, g2, g3s, g3, g4, g5, send, recv,
    ):
        row = lax.axis_index("row")
        p = lax.axis_index("rep")
        z = row // ny
        y = row - z * ny

        def on_rep(q):
            return (row, q)

        def on_z(q):
            return (q * ny + y, p)

        def on_y(q):
            return (z * ny + q, p)

        axes = ((nrep, p, on_rep), (nz, z, on_z), (ny, y, on_y))
        rep_axis, z_axis, y_axis = axes

        def others(axis):
            n, me, dev = axis
            order = []
            for d in range(1, n // 2 + 1):
                order.append(d)
                if n - d != d:
                    order.append(n - d)
            return [lax.rem(me + d, n) for d in order]

        def send_to(axis, t, src, dst, sem, left=None):
            pltpu.make_async_remote_copy(
                src_ref=src, dst_ref=dst, recv_sem=recv.at[sem],
                send_sem=send.at[sem if left is None else left],
                device_id=axis[2](t), device_id_type=MESH,
            ).start()

        def wait_bytes(ref, sem):
            pltpu.make_async_copy(ref, ref, sem).wait()

        def most(buf, n):
            return buf.at[pl.ds(0, n - 1)]

        barrier = pltpu.get_barrier_semaphore()
        count = 0
        for axis in axes:
            for t in others(axis):
                pl.semaphore_signal(barrier, inc=1, device_id=axis[2](t), device_id_type=MESH)
                count += 1

        lane = lax.broadcasted_iota(jnp.int32, (8, tiles_all), 1)
        code = jnp.zeros((8, tiles_all), jnp.int32)
        for k in range(tpd):
            own = owner[k, 0]
            own_z = own // ny
            own_y = own - own_z * ny
            b = tblock[k]
            low = b - (b // half) * half
            first = own_y * (2 * nz) + own_z * half + low
            second = hpos + own_z * (2 * ny) + own_y * half + low
            where_to = jnp.where(b < half, first, second) + trow[k] * npos
            code = jnp.where(lane == p * tpd + k, where_to, code)
        meta_s[...] = code

        pl.semaphore_wait(barrier, count)

        start = pl.multiple_of(p * cs, cs)
        f1[0, z] = feat[pl.ds(0, half), pl.ds(start, cs), :]
        f1[1, y] = feat[pl.ds(half, half), pl.ds(start, cs), :]
        for h, axis in ((0, z_axis), (1, y_axis)):
            for t in others(axis):
                send_to(axis, t, feat.at[pl.ds(h * half, half), pl.ds(start, cs), :],
                        f1.at[h, axis[1]], 2 + h)
        for t in others(rep_axis):
            send_to(rep_axis, t, meta_s, meta.at[p], 0)
        meta[p] = code

        for k in range(tpd):
            xt[k] = tiles[k].T
        tile_swap = swap_matrix(tpd, cs)
        node_swap = swap_matrix(nz * half, cs)

        def columns_of(t):
            part = xt[:, pl.ds(pl.multiple_of(t * cs, cs), cs), :].reshape(tpd * cs, blk)
            return dot(tile_swap, part).astype(BF).reshape(cs, tpd, blk)

        for t in others(rep_axis):
            ysend[t] = columns_of(t)
            send_to(rep_axis, t, ysend.at[t], tt.at[p], 1)
        tt[p] = columns_of(p)

        for h, axis in ((0, y_axis), (1, z_axis)):
            wait_bytes(most(f1.at[h], nz), recv.at[2 + h])
            part = dot(node_swap, f1[h].reshape(hpos // ny * cs, width)).astype(BF)
            f2[h, axis[1]] = part.reshape(cs, nz * half, width)
            for t in others(axis):
                send_to(axis, t, f2.at[h, axis[1]], f2.at[h, axis[1]], 4 + h)

        wait_bytes(most(meta, nrep), recv.at[0])
        codes = meta[0]
        for q in range(1, nrep):
            codes = codes + meta[q]
        codes = codes[0:1, :]
        rows_of = codes // npos
        pos = codes - rows_of * npos
        wait_bytes(most(tt, nrep), recv.at[1])
        for c in range(cs):
            turned = tt[:, c].reshape(tiles_all, blk).T
            for n in range(nbd):
                ttm[n * blk:(n + 1) * blk, c * tiles_all:(c + 1) * tiles_all] = jnp.where(
                    rows_of == n, turned, jnp.zeros_like(turned))
        pos_iota = lax.broadcasted_iota(jnp.int32, (npos, tiles_all), 0)
        select = (pos_iota == pos).astype(F32).T.astype(BF)

        for h in range(2):
            wait_bytes(most(f2.at[h], ny), recv.at[4 + h])
        for c in range(cs):
            here = jnp.concatenate(
                [f2[0, :, c].reshape(hpos, width), f2[1, :, c].reshape(hpos, width)], axis=0)
            fg[c * tiles_all:(c + 1) * tiles_all, :] = dot(select, here).astype(BF)
        partial = dot(ttm[...], fg[...]).astype(BF).reshape(nrep, share, width)
        a0[...] = partial
        for t in others(rep_axis):
            send_to(rep_axis, t, a0.at[t], a1.at[p], 6)
        a1[p] = a0[p]

        spread = jnp.concatenate(
            [(pos_iota + n * npos == codes).astype(F32).astype(BF) for n in range(nbd)], axis=0)
        for c in range(cs):
            placed = dot(spread, tt[:, c].reshape(tiles_all, blk)).astype(BF)
            for n in range(nbd):
                dense[c, :, n * blk:(n + 1) * blk] = placed[n * npos:(n + 1) * npos]

        per_block = blk // share if share < blk else 1
        if share < blk:
            which = p // per_block
            inside = pl.multiple_of((p - which * per_block) * share, share)
            own = feat[which, pl.ds(inside, share), :]
        else:
            own = feat[pl.ds(p * (share // blk), share // blk)].reshape(share, width)
        own_part = dot(own, w_self[...]) + bias[...]

        wait_bytes(most(a1, nrep), recv.at[6])
        total = a1[0].astype(F32)
        for q in range(1, nrep):
            total = total + a1[q].astype(F32)
        agg = total.astype(BF)
        pre = own_part + dot(agg, w_neigh[...])
        sig = jax.nn.sigmoid(pre)
        dpre = cot[...].astype(F32) * sig * (1.0 + pre * (1.0 - sig))
        dpre_b = dpre.astype(BF)
        contract_cols = (((1,), (1,)), ((), ()))
        dagg = lax.dot_general(dpre_b, w_neigh[...], contract_cols, preferred_element_type=F32)
        dg0[...] = dagg.astype(BF)
        for t in others(rep_axis):
            send_to(rep_axis, t, dg0, dg.at[p], 7)
        dg[p] = dg0[...]
        hid_o[...] = (pre * sig).astype(BF)

        contract_rows = (((0,), (0,)), ((), ()))
        bsum = jnp.sum(dpre, axis=0, keepdims=True)
        row8 = lax.broadcasted_iota(jnp.int32, (8, width), 0)
        bias_rows = jnp.where(row8 == 0, bsum[:, :width],
                              jnp.where(row8 == 1, bsum[:, width:], 0.0))
        both = jnp.concatenate([own, agg], axis=1)
        grads = lax.dot_general(both, dpre_b, contract_rows, preferred_element_type=F32)
        pieces = jnp.concatenate(
            [grads[w * width:(w + 1) * width, s * width:(s + 1) * width]
             for w in range(2) for s in range(2)], axis=0)
        for q in range(nrep):
            gl[q, 0:wrows, :] = pieces[q * wrows:(q + 1) * wrows]
            gl[q, wrows:wrows + 8, :] = bias_rows
        for t in others(rep_axis):
            send_to(rep_axis, t, gl.at[t], g1.at[p], 13)
        g1[p] = gl[p]

        wait_bytes(most(dg, nrep), recv.at[7])
        dall = dg[...].reshape(nodes, width)
        for c in range(cs):
            made = dot(dense[c], dall).astype(BF)
            o0[0, :, c] = made[:hpos].reshape(ny, nz * half, width)
            o0[1, :, c] = made[hpos:].reshape(nz, ny * half, width)
        for h, axis in ((0, y_axis), (1, z_axis)):
            for t in others(axis):
                send_to(axis, t, o0.at[h, t], b1.at[h, axis[1]], 8 + h)
            b1[h, axis[1]] = o0[h, axis[1]]

        def summed(buf, n):
            acc = buf[0]
            for q in range(1, n):
                acc = acc + buf[q]
            return acc

        wait_bytes(most(g1, nrep), recv.at[13])
        gsum = summed(g1, nrep)
        for q in range(ny):
            g2s[q, 0:yrows, :] = gsum[q * yrows:(q + 1) * yrows]
            g2s[q, yrows:yrows + 8, :] = gsum[wrows:]
        for t in others(y_axis):
            send_to(y_axis, t, g2s.at[t], g2.at[y], 14)
        g2[y] = g2s[y]
        wait_bytes(most(g2, ny), recv.at[14])
        g3s[...] = summed(g2, ny)
        for t in others(z_axis):
            send_to(z_axis, t, g3s, g3.at[z], 15)
        g3[z] = g3s[...]

        for h, axis in ((0, z_axis), (1, y_axis)):
            wait_bytes(most(b1.at[h], ny), recv.at[8 + h])
            acc = b1[h, 0].astype(F32)
            for q in range(1, ny):
                acc = acc + b1[h, q].astype(F32)
            acc = acc.reshape(hpos // ny * cs, width).astype(BF)
            back_swap = node_swap if cs == nz * half else swap_matrix(cs, nz * half)
            b2s[h] = dot(back_swap, acc).astype(BF).reshape(nz, half, cs, width)
            for t in others(axis):
                send_to(axis, t, b2s.at[h, t], b2.at[h, axis[1]], 10 + h)
            b2[h, axis[1]] = b2s[h, axis[1]]

        wait_bytes(most(g3, nz), recv.at[15])
        gfull = summed(g3, nz) * scale
        gb_o[...] = jnp.concatenate([gfull[yrows:yrows + 1], gfull[yrows + 1:yrows + 2]], axis=1)
        g4[y] = gfull[:yrows]
        for t in others(y_axis):
            send_to(y_axis, t, g4.at[y], g4.at[y], 16)

        for h in range(2):
            wait_bytes(most(b2.at[h], nz), recv.at[10 + h])
            acc = b2[h, 0].astype(F32)
            for q in range(1, nz):
                acc = acc + b2[h, q].astype(F32)
            r0[pl.ds(h * half, half)] = acc
        for b in range(nbd):
            node = b * blk + p * cs
            to = node // share
            slot = (node - to * share) // cs

            @pl.when(to == p)
            def _():
                pltpu.make_async_copy(r0.at[b], r1.at[slot], recv.at[12]).start()

            @pl.when(to != p)
            def _():
                send_to(rep_axis, to, r0.at[b], r1.at[slot], 12, 18 + b)

        wait_bytes(most(g4, ny), recv.at[16])
        g5[p] = g4[...].reshape(wrows, width)
        for t in others(rep_axis):
            send_to(rep_axis, t, g5.at[p], g5.at[p], 17)

        contract = lax.dot_general(dpre_b, w_self[...], contract_cols, preferred_element_type=F32)
        wait_bytes(r1, recv.at[12])
        gf_o[...] = contract + r1[...].reshape(share, width)
        wait_bytes(most(g5, nrep), recv.at[17])
        every = g5[...].reshape(4, width, width)
        for s in range(2):
            gs_o[:, s * width:(s + 1) * width] = every[s]
            gn_o[:, s * width:(s + 1) * width] = every[2 + s]

        wait_bytes(most(meta, nrep), send.at[0])
        wait_bytes(most(tt, nrep), send.at[1])
        for h in range(2):
            wait_bytes(most(f1.at[h], nz), send.at[2 + h])
            wait_bytes(most(f2.at[h], nz), send.at[4 + h])
            wait_bytes(most(b1.at[h], nz), send.at[8 + h])
            wait_bytes(most(b2.at[h], nz), send.at[10 + h])
        wait_bytes(most(a1, nrep), send.at[6])
        wait_bytes(most(dg, nrep), send.at[7])
        for b in range(nbd):
            node = b * blk + p * cs

            @pl.when(node // share != p)
            def _():
                wait_bytes(r0.at[b], send.at[18 + b])
        wait_bytes(most(g1, nrep), send.at[13])
        wait_bytes(most(g2, ny), send.at[14])
        wait_bytes(most(g3, nz), send.at[15])
        wait_bytes(most(g4, ny), send.at[16])
        wait_bytes(most(g5, nrep), send.at[17])

    V = pltpu.VMEM
    scratch = [
        V((8, tiles_all), jnp.int32),
        V((nrep, 8, tiles_all), jnp.int32),
        V((tpd, blk, blk), BF),
        V((nrep, cs, tpd, blk), BF),
        V((nrep, cs, tpd, blk), BF),
        V((2, nz, half, cs, width), BF),
        V((2, ny, cs, nz * half, width), BF),
        V((nodes, cs * tiles_all), BF),
        V((cs * tiles_all, width), BF),
        V((nrep, share, width), BF),
        V((nrep, share, width), BF),
        V((cs, npos, nodes), BF),
        V((share, width), BF),
        V((nrep, share, width), BF),
        V((2, ny, cs, nz * half, width), BF),
        V((2, ny, cs, nz * half, width), BF),
        V((2, nz, half, cs, width), BF),
        V((2, nz, half, cs, width), BF),
        V((nbd, cs, width), F32),
        V((share // cs, cs, width), F32),
        V((nrep, wrows + 8, width), F32),
        V((nrep, wrows + 8, width), F32),
        V((ny, yrows + 8, width), F32),
        V((ny, yrows + 8, width), F32),
        V((yrows + 8, width), F32),
        V((nz, yrows + 8, width), F32),
        V((ny, yrows, width), F32),
        V((nrep, wrows, width), F32),
        pltpu.SemaphoreType.DMA((22,)),
        pltpu.SemaphoreType.DMA((18,)),
    ]
    outs = (
        jax.ShapeDtypeStruct((share, hid), BF),
        jax.ShapeDtypeStruct((share, width), F32),
        jax.ShapeDtypeStruct((width, hid), F32),
        jax.ShapeDtypeStruct((width, hid), F32),
        jax.ShapeDtypeStruct((1, hid), F32),
    )
    vmem, smem = pl.BlockSpec(memory_space=pltpu.VMEM), pl.BlockSpec(memory_space=pltpu.SMEM)
    return pl.pallas_call(
        kernel,
        out_shape=outs,
        in_specs=[vmem, vmem, smem, smem, smem, vmem, vmem, vmem, vmem],
        out_specs=tuple([vmem] * 5),
        scratch_shapes=scratch,
        compiler_params=pltpu.CompilerParams(
            collective_id=0, has_side_effects=True, vmem_limit_bytes=56 * 1024 * 1024),
    )


def solution(mesh):
    nrow, nrep = mesh.shape["row"], mesh.shape["rep"]
    side = int(round(nrow ** 0.5))

    def per_device(features, edge_tiles, tile_owner, tile_block, tile_row, w_self, w_neigh,
                   bias_vector, cotangent):
        tpd, blk, _ = edge_tiles.shape
        nodes, width = features.shape
        hid = w_self.shape[1]
        nbd = nodes // blk
        call = make_kernel(side, nrow // side, nrep, tpd, blk, width, hid, nbd)
        hidden, gf, gs, gn, gb = call(
            features.reshape(nbd, blk, width), edge_tiles, tile_owner, tile_block, tile_row,
            w_self, w_neigh, bias_vector.reshape(1, hid), cotangent)
        return hidden, gf, gs, gn, gb.reshape(hid)

    in_specs = (
        P("row", None), P(("row", "rep"), None, None), P(("row", "rep"), None),
        P(("row", "rep")), P(("row", "rep")), P(), P(), P(), P(("row", "rep"), None),
    )
    out_specs = (P(("row", "rep"), None), P(("row", "rep"), None), P(), P(), P())
    return jax.shard_map(
        per_device, mesh=mesh, in_specs=in_specs, out_specs=out_specs, check_vma=False)
```

time: 588 us -> 85.7 us (0.15)
  blocking collectives: 265 us -> 0 us
  waiting for transfers between devices: 235 us -> 0 us
  Pallas kernels: 0 us -> 78.5 us
  starting transfers between devices: 27.3 us -> 0 us
  local copies, waits for them, and re-layouts: 29.3 us -> 6.29 us
  between operations: 14 us -> 0.66 us
  matrix products: 8.03 us -> 0 us
  other arithmetic: 6.57 us -> 0 us
    psum x2 -> x0, blocking collectives: 249 us -> none  [the longest x1 224 us: per_device(): lax.psum((local_self, local_neigh, local_bias), ('row', 'rep'))]
    psum x1 -> x0, waiting for transfers between devices: 118 us -> none  [per_device(): lax.psum((local_self, local_neigh, local_bias), ('row', 'rep'))]
    all_gather x1 -> x0, waiting for transfers between devices: 84.8 us -> none  [per_device(): gathered = lax.all_gather(features, 'row', axis=0, tiled=True)]
    pallas_call x0 -> x1, Pallas kernels: none -> 78.5 us  [per_device(): call(features.reshape(nbd, blk, width), edge_tiles, tile_owner, tile_bloc...]
    reduce_scatter x1 -> x0, waiting for transfers between devices: 31.7 us -> none  [per_device(): lax.psum_scatter(back_partial.astype(jnp.bfloat16), 'rep', scatter_dimens...]
    all_to_all x2 -> x0, starting transfers between devices: 27.2 us -> none  [the longest x1 17.1 us: per_device(): lax.all_to_all(request, 'row', split_axis=0, concat_axis=0, tiled=True)]
    all_gather x1 -> x0, blocking collectives: 16.3 us -> none  [per_device(): lax.all_gather(dagg, 'rep', axis=0, tiled=True)]
    reshape x1 -> x0, local copies, waits for them, and re-layouts: 8.48 us -> none  [per_device(): outgoing.reshape(row_count, capacity, block_size, width)]
  transfers between devices with their start and end apart: 5 -> 0, of which waited for: 3 -> 0; matrix products, arithmetic and copies ran while one was open for 7% -> 0% of each run, Pallas kernels for 0% -> 0%
where the time goes in v1:
time: 85.7 us; the launch traced here: 85.5 us
  Pallas kernels  78.5 us (92%)
  local copies, waits for them, and re-layouts  6.29 us (7%)
    pallas_call x1, Pallas kernels, per_device(): call(features.reshape(nbd, blk, width), edge_tiles, tile_owner, tile_bloc...  78.5 us
    unnamed x14, local copies, waits for them, and re-layouts  6.29 us

profile of v1, /device:TPU:1, one launch (start us, length us, event | category | flops | bytes accessed | tf_op | source)
XLA Modules:
  0.0 85.5 jit_solution(264301564386971051)
XLA Ops:
  0.6 0.0 copy-start.3
  0.6 0.6 copy-done.3
  1.3 0.7 copy.14.owner
  2.0 78.5 %shard_map.128 = (bf16[64,256]{1,0:T(8,128)(2,1)}, f32[64,128]{1,0:T(8,128)}, f32[128,256]{1,0:T(8,128)}, f32[128,256]{1,0:T(8,128)}, f32[1,256]{1,0:T(1,128)}) custom-call(bf16[4,128,128]{2,1,0:T(8,128)(2,1)} %bitcast.3, bf16[16,128,128]{2,1,0:T(8,128)(2,1)} %tiles.1, s32[16,1]{1,0:T(8,128)} %copy.14.owner, s32[16]{0:T(128)} %tblock.1, s32[16]{0:T(128)} %trow.1, ...), custom_call_target="tpu_custom_call" | custom-call | tf_op jit(solution)/shard_map/pallas_call | solution.py:383
  80.5 0.0 copy-start.1
  80.5 1.4 %copy.20 = bf16[64,256]{1,0:T(8,128)(2,1)} copy(bf16[64,256]{1,0:T(8,128)(2,1)} %get-tuple-element.20) | data formatting | bytes 65536
  81.9 1.4 %copy.21 = f32[64,128]{1,0:T(8,128)} copy(f32[64,128]{1,0:T(8,128)} %get-tuple-element.21) | data formatting | bytes 65536
  83.3 0.0 copy-done.1
  83.3 0.0 copy-start
  83.3 0.7 copy.22
  84.0 0.3 copy-done
  84.3 0.0 copy-start.2
  84.3 0.7 copy.23
  84.9 0.0 copy-done.2
  84.9 0.6 copy.24
Async XLA Ops:
  0.6 0.7 copy-start.3
  80.5 2.8 %copy-start.1 = (f32[128,256]{1,0:T(8,128)S(1)}, f32[128,256]{1,0:T(8,128)}, u32[]{:S(2)}) copy-start(f32[128,256]{1,0:T(8,128)} %get-tuple-element.22) | copy-start | bytes 393220
  83.3 1.0 %copy-start = (f32[128,256]{1,0:T(8,128)S(1)}, f32[128,256]{1,0:T(8,128)}, u32[]{:S(2)}) copy-start(f32[128,256]{1,0:T(8,128)} %get-tuple-element.23) | copy-start | bytes 393220
  84.3 0.7 copy-start.2

commit v2 on v1

--- a/solution.py
+++ b/solution.py
@@ -34,12 +34,14 @@
     assert nz == ny and hid == 2 * width
     wrows = 4 * width // nrep
     yrows = wrows // ny
+    early = min(3, ny - 1)
+    nx = nrep // 2
 
     def kernel(
         feat, tiles, owner, tblock, trow, w_self, w_neigh, bias, cot,
         hid_o, gf_o, gs_o, gn_o, gb_o,
         meta_s, meta, xt, ysend, tt, f1, f2, ttm, fg, a0, a1, dense, dg0, dg, o0, b1, b2s, b2,
-        r0, r1, gl, g1, g2s, g2, g3s, g3, g4, g5, send, recv,
+        gl, g1, g2s, g2, g3s, g3, g4, g5, send, recv,
     ):
         row = lax.axis_index("row")
         p = lax.axis_index("rep")
@@ -58,14 +60,20 @@
         axes = ((nrep, p, on_rep), (nz, z, on_z), (ny, y, on_y))
         rep_axis, z_axis, y_axis = axes
 
+        def far_first(n):
+            order = []
+            for d in range(n // 2, 0, -1):
+                order += [d] if n - d == d else [d, n - d]
+            return order
+
         def others(axis):
-            n, me, dev = axis
-            order = []
-            for d in range(1, n // 2 + 1):
-                order.append(d)
-                if n - d != d:
-                    order.append(n - d)
-            return [lax.rem(me + d, n) for d in order]
+            n, me, _ = axis
+            if axis is rep_axis:
+                x = me // 2
+                core = me - 2 * x
+                return [lax.rem(x + d, nx) * 2 + lax.rem(core + e, 2)
+                        for d in far_first(nx) + [0] for e in (0, 1) if d or e]
+            return [lax.rem(me + d, n) for d in far_first(n)]
 
         def send_to(axis, t, src, dst, sem, left=None):
             pltpu.make_async_remote_copy(
@@ -90,7 +98,7 @@
         lane = lax.broadcasted_iota(jnp.int32, (8, tiles_all), 1)
         code = jnp.zeros((8, tiles_all), jnp.int32)
         for k in range(tpd):
-            own = owner[k, 0]
+            own = owner[k]
             own_z = own // ny
             own_y = own - own_z * ny
             b = tblock[k]
@@ -168,7 +176,10 @@
         for c in range(cs):
             placed = dot(spread, tt[:, c].reshape(tiles_all, blk)).astype(BF)
             for n in range(nbd):
-                dense[c, :, n * blk:(n + 1) * blk] = placed[n * npos:(n + 1) * npos]
+                for h in range(2):
+                    at = n * npos + h * hpos
+                    dense[h, :, c, :, n * blk:(n + 1) * blk] = placed[at:at + hpos].reshape(
+                        ny, nz * half, blk)
 
         per_block = blk // share if share < blk else 1
         if share < blk:
@@ -198,64 +209,69 @@
 
         contract_rows = (((0,), (0,)), ((), ()))
         bsum = jnp.sum(dpre, axis=0, keepdims=True)
-        row8 = lax.broadcasted_iota(jnp.int32, (8, width), 0)
-        bias_rows = jnp.where(row8 == 0, bsum[:, :width],
-                              jnp.where(row8 == 1, bsum[:, width:], 0.0))
+        high = bsum.astype(BF).astype(F32)
+        row16 = lax.broadcasted_iota(jnp.int32, (16, width), 0)
+        bias_rows = jnp.zeros((16, width), F32)
+        for at, part in ((0, high), (8, bsum - high)):
+            for s in range(2):
+                bias_rows = jnp.where(row16 == at + s, part[:, s * width:(s + 1) * width], bias_rows)
+        bias_rows = bias_rows.astype(BF)
         both = jnp.concatenate([own, agg], axis=1)
         grads = lax.dot_general(both, dpre_b, contract_rows, preferred_element_type=F32)
         pieces = jnp.concatenate(
             [grads[w * width:(w + 1) * width, s * width:(s + 1) * width]
              for w in range(2) for s in range(2)], axis=0)
         for q in range(nrep):
-            gl[q, 0:wrows, :] = pieces[q * wrows:(q + 1) * wrows]
-            gl[q, wrows:wrows + 8, :] = bias_rows
+            gl[q, 0:wrows, :] = pieces[q * wrows:(q + 1) * wrows].astype(BF)
+            gl[q, wrows:wrows + 16, :] = bias_rows
         for t in others(rep_axis):
             send_to(rep_axis, t, gl.at[t], g1.at[p], 13)
         g1[p] = gl[p]
 
+        def summed(buf, n):
+            acc = buf[0].astype(F32)
+            for q in range(1, n):
+                acc = acc + buf[q].astype(F32)
+            return acc
+
         wait_bytes(most(dg, nrep), recv.at[7])
         dall = dg[...].reshape(nodes, width)
-        for c in range(cs):
-            made = dot(dense[c], dall).astype(BF)
-            o0[0, :, c] = made[:hpos].reshape(ny, nz * half, width)
-            o0[1, :, c] = made[hpos:].reshape(nz, ny * half, width)
-        for h, axis in ((0, y_axis), (1, z_axis)):
-            for t in others(axis):
-                send_to(axis, t, o0.at[h, t], b1.at[h, axis[1]], 8 + h)
-            b1[h, axis[1]] = o0[h, axis[1]]
-
-        def summed(buf, n):
-            acc = buf[0]
-            for q in range(1, n):
-                acc = acc + buf[q]
-            return acc
+        by_half = ((0, y_axis), (1, z_axis))
+
+        def back_piece(h, t):
+            flat = dense[h, t].reshape(cs * nz * half, nodes)
+            return dot(flat, dall).astype(BF).reshape(cs, nz * half, width)
+
+        def back_send(first, last):
+            for i in range(first, last):
+                for h, axis in by_half:
+                    t = others(axis)[i]
+                    o0[h, t] = back_piece(h, t)
+                    send_to(axis, t, o0.at[h, t], b1.at[h, axis[1]], 8 + h)
+
+        back_send(0, 1)
 
         wait_bytes(most(g1, nrep), recv.at[13])
         gsum = summed(g1, nrep)
+        gbias = gsum[wrows:wrows + 8] + gsum[wrows + 8:wrows + 16]
         for q in range(ny):
             g2s[q, 0:yrows, :] = gsum[q * yrows:(q + 1) * yrows]
-            g2s[q, yrows:yrows + 8, :] = gsum[wrows:]
+            g2s[q, yrows:yrows + 8, :] = gbias
         for t in others(y_axis):
             send_to(y_axis, t, g2s.at[t], g2.at[y], 14)
         g2[y] = g2s[y]
+        back_send(1, early)
+
         wait_bytes(most(g2, ny), recv.at[14])
         g3s[...] = summed(g2, ny)
         for t in others(z_axis):
             send_to(z_axis, t, g3s, g3.at[z], 15)
         g3[z] = g3s[...]
-
-        for h, axis in ((0, z_axis), (1, y_axis)):
-            wait_bytes(most(b1.at[h], ny), recv.at[8 + h])
-            acc = b1[h, 0].astype(F32)
-            for q in range(1, ny):
-                acc = acc + b1[h, q].astype(F32)
-            acc = acc.reshape(hpos // ny * cs, width).astype(BF)
-            back_swap = node_swap if cs == nz * half else swap_matrix(cs, nz * half)
-            b2s[h] = dot(back_swap, acc).astype(BF).reshape(nz, half, cs, width)
-            for t in others(axis):
-                send_to(axis, t, b2s.at[h, t], b2.at[h, axis[1]], 10 + h)
-            b2[h, axis[1]] = b2s[h, axis[1]]
-
+        back_send(early, ny - 1)
+        for h, axis in by_half:
+            b1[h, axis[1]] = back_piece(h, axis[1])
+
+        contract = lax.dot_general(dpre_b, w_self[...], contract_cols, preferred_element_type=F32)
         wait_bytes(most(g3, nz), recv.at[15])
         gfull = summed(g3, nz) * scale
         gb_o[...] = jnp.concatenate([gfull[yrows:yrows + 1], gfull[yrows + 1:yrows + 2]], axis=1)
@@ -263,35 +279,45 @@
         for t in others(y_axis):
             send_to(y_axis, t, g4.at[y], g4.at[y], 16)
 
-        for h in range(2):
-            wait_bytes(most(b2.at[h], nz), recv.at[10 + h])
-            acc = b2[h, 0].astype(F32)
-            for q in range(1, nz):
-                acc = acc + b2[h, q].astype(F32)
-            r0[pl.ds(h * half, half)] = acc
-        for b in range(nbd):
-            node = b * blk + p * cs
-            to = node // share
-            slot = (node - to * share) // cs
-
-            @pl.when(to == p)
-            def _():
-                pltpu.make_async_copy(r0.at[b], r1.at[slot], recv.at[12]).start()
-
-            @pl.when(to != p)
-            def _():
-                send_to(rep_axis, to, r0.at[b], r1.at[slot], 12, 18 + b)
+        back_swap = node_swap if cs == nz * half else swap_matrix(cs, nz * half)
+        for h, axis in ((0, z_axis), (1, y_axis)):
+            wait_bytes(most(b1.at[h], ny), recv.at[8 + h])
+            acc = summed(b1.at[h], ny).reshape(hpos // ny * cs, width).astype(BF)
+            b2s[h] = dot(back_swap, acc).astype(BF).reshape(nz, half, cs, width)
+            for t in others(axis) + [None]:
+                for low in range(half):
+                    b = h * half + low
+                    node = b * blk + p * cs
+                    to = node // share
+                    slot = (node - to * share) // cs
+                    into = b2.at[axis[1], slot]
+                    if t is not None:
+                        place = (t * ny + y, to) if h == 0 else (z * ny + t, to)
+                        pltpu.make_async_remote_copy(
+                            src_ref=b2s.at[h, t, low], dst_ref=into, send_sem=send.at[10],
+                            recv_sem=recv.at[10], device_id=place, device_id_type=MESH,
+                        ).start()
+                        continue
+
+                    mine = b2s.at[h, axis[1], low]
+
+                    @pl.when(to == p)
+                    def _():
+                        pltpu.make_async_copy(mine, into, recv.at[10]).start()
+
+                    @pl.when(to != p)
+                    def _():
+                        send_to(rep_axis, to, mine, into, 10, 18 + b)
 
         wait_bytes(most(g4, ny), recv.at[16])
-        g5[p] = g4[...].reshape(wrows, width)
+        g5[p] = g4[...].reshape(wrows, width).astype(BF)
         for t in others(rep_axis):
             send_to(rep_axis, t, g5.at[p], g5.at[p], 17)
 
-        contract = lax.dot_general(dpre_b, w_self[...], contract_cols, preferred_element_type=F32)
-        wait_bytes(r1, recv.at[12])
-        gf_o[...] = contract + r1[...].reshape(share, width)
+        wait_bytes(b2, recv.at[10])
+        gf_o[...] = contract + summed(b2, nz).reshape(share, width)
         wait_bytes(most(g5, nrep), recv.at[17])
-        every = g5[...].reshape(4, width, width)
+        every = g5[...].reshape(4, width, width).astype(F32)
         for s in range(2):
             gs_o[:, s * width:(s + 1) * width] = every[s]
             gn_o[:, s * width:(s + 1) * width] = every[2 + s]
@@ -302,15 +328,15 @@
             wait_bytes(most(f1.at[h], nz), send.at[2 + h])
             wait_bytes(most(f2.at[h], nz), send.at[4 + h])
             wait_bytes(most(b1.at[h], nz), send.at[8 + h])
-            wait_bytes(most(b2.at[h], nz), send.at[10 + h])
         wait_bytes(most(a1, nrep), send.at[6])
         wait_bytes(most(dg, nrep), send.at[7])
+        wait_bytes(most(b2, nz), send.at[10])
         for b in range(nbd):
             node = b * blk + p * cs
 
             @pl.when(node // share != p)
             def _():
-                wait_bytes(r0.at[b], send.at[18 + b])
+                wait_bytes(b2s.at[0, 0, 0], send.at[18 + b])
         wait_bytes(most(g1, nrep), send.at[13])
         wait_bytes(most(g2, ny), send.at[14])
         wait_bytes(most(g3, nz), send.at[15])
@@ -330,23 +356,21 @@
         V((cs * tiles_all, width), BF),
         V((nrep, share, width), BF),
         V((nrep, share, width), BF),
-        V((cs, npos, nodes), BF),
+        V((2, ny, cs, nz * half, nodes), BF),
         V((share, width), BF),
         V((nrep, share, width), BF),
         V((2, ny, cs, nz * half, width), BF),
         V((2, ny, cs, nz * half, width), BF),
         V((2, nz, half, cs, width), BF),
-        V((2, nz, half, cs, width), BF),
-        V((nbd, cs, width), F32),
-        V((share // cs, cs, width), F32),
-        V((nrep, wrows + 8, width), F32),
-        V((nrep, wrows + 8, width), F32),
+        V((nz, share // cs, cs, width), BF),
+        V((nrep, wrows + 16, width), BF),
+        V((nrep, wrows + 16, width), BF),
         V((ny, yrows + 8, width), F32),
         V((ny, yrows + 8, width), F32),
         V((yrows + 8, width), F32),
         V((nz, yrows + 8, width), F32),
         V((ny, yrows, width), F32),
-        V((nrep, wrows, width), F32),
+        V((nrep, wrows, width), BF),
         pltpu.SemaphoreType.DMA((22,)),
         pltpu.SemaphoreType.DMA((18,)),
     ]
@@ -369,6 +393,25 @@
     )
 
 
+def finish(results):
+    def kernel(*refs):
+        n = len(results)
+        copies = [pltpu.make_async_copy(refs[i], refs[n + i], refs[2 * n].at[i]) for i in range(n)]
+        for copy in copies:
+            copy.start()
+        for copy in copies:
+            copy.wait()
+
+    anywhere = pl.BlockSpec(memory_space=pl.ANY)
+    return pl.pallas_call(
+        kernel,
+        out_shape=tuple(jax.ShapeDtypeStruct(r.shape, r.dtype) for r in results),
+        in_specs=[pl.BlockSpec(memory_space=pltpu.VMEM)] * len(results),
+        out_specs=tuple([anywhere] * len(results)),
+        scratch_shapes=[pltpu.SemaphoreType.DMA((len(results),))],
+    )(*results)
+
+
 def solution(mesh):
     nrow, nrep = mesh.shape["row"], mesh.shape["rep"]
     side = int(round(nrow ** 0.5))
@@ -380,9 +423,10 @@
         hid = w_self.shape[1]
         nbd = nodes // blk
         call = make_kernel(side, nrow // side, nrep, tpd, blk, width, hid, nbd)
-        hidden, gf, gs, gn, gb = call(
-            features.reshape(nbd, blk, width), edge_tiles, tile_owner, tile_block, tile_row,
+        results = call(
+            features.reshape(nbd, blk, width), edge_tiles, tile_owner.reshape(tpd), tile_block, tile_row,
             w_self, w_neigh, bias_vector.reshape(1, hid), cotangent)
+        hidden, gf, gs, gn, gb = finish(results)
         return hidden, gf, gs, gn, gb.reshape(hid)
 
     in_specs = (

time: 85.7 us -> 70.3 us (0.82)
  Pallas kernels: 78.5 us -> 69.5 us
  local copies, waits for them, and re-layouts: 6.29 us -> 0 us
    pallas_call x1 -> x2, Pallas kernels: 78.5 us -> 69.5 us  [the longest x1 67.7 us: per_device(): call(features.reshape(nbd, blk, width), edge_tiles, tile_owner.reshape(tp...]
    unnamed x14 -> x0, local copies, waits for them, and re-layouts: 6.29 us -> none
where the time goes in v2:
time: 70.3 us; the launch traced here: 70.2 us
  Pallas kernels  69.5 us (99%)
    pallas_call x1, Pallas kernels, per_device(): call(features.reshape(nbd, blk, width), edge_tiles, tile_owner.reshape(tp...  67.7 us
    pallas_call x1, Pallas kernels, finish(): pl.pallas_call(kernel, out_shape=tuple((jax.ShapeDtypeStruct(r.shape, r.d...  1.78 us

profile of v2, /device:TPU:1, one launch (start us, length us, event | category | flops | bytes accessed | tf_op | source)
XLA Modules:
  0.0 70.2 jit_solution(14239272015245967588)
XLA Ops:
  0.6 67.7 %shard_map.128 = (bf16[64,256]{1,0:T(8,128)(2,1)}, f32[64,128]{1,0:T(8,128)}, f32[128,256]{1,0:T(8,128)}, f32[128,256]{1,0:T(8,128)}, f32[1,256]{1,0:T(1,128)}) custom-call(bf16[4,128,128]{2,1,0:T(8,128)(2,1)} %bitcast.4, bf16[16,128,128]{2,1,0:T(8,128)(2,1)} %tiles.1, s32[16]{0:T(128)} %bitcast.6, s32[16]{0:T(128)} %tblock.1, s32[16]{0:T(128)} %trow.1, ...), custom_call_target="tpu_custom_call" | custom-call | tf_op jit(solution)/shard_map/pallas_call | solution.py:426
  68.4 1.8 %shard_map.129 = (bf16[64,256]{1,0:T(8,128)(2,1)}, f32[64,128]{1,0:T(8,128)}, f32[128,256]{1,0:T(8,128)}, f32[128,256]{1,0:T(8,128)}, f32[1,256]{1,0:T(1,128)}) custom-call(bf16[64,256]{1,0:T(8,128)(2,1)} %get-tuple-element.15.refs_0_, f32[64,128]{1,0:T(8,128)} %get-tuple-element.16.refs_1_, f32[128,256]{1,0:T(8,128)} %get-tuple-element.17.refs_2_, ...), custom_call_target="tpu_custom_call" | custom-call | tf_op jit(solution)/shard_map/pallas_call | solution.py:406

commit v3 on v2

--- a/solution.py
+++ b/solution.py
@@ -31,17 +31,17 @@
     hpos = npos // 2
     tiles_all = nrep * tpd
     scale = float(nz * ny * nodes) ** -0.5
-    assert nz == ny and hid == 2 * width
-    wrows = 4 * width // nrep
-    yrows = wrows // ny
-    early = min(3, ny - 1)
+    assert nz == ny == 8 and hid == 2 * width
+    grows = 2 * width // ny
+    F2, P2, M2, B1, RL, RP, RM, GA, GB, GD = range(20, 40, 2)
+    GC = 13
     nx = nrep // 2
 
     def kernel(
         feat, tiles, owner, tblock, trow, w_self, w_neigh, bias, cot,
         hid_o, gf_o, gs_o, gn_o, gb_o,
         meta_s, meta, xt, ysend, tt, f1, f2, ttm, fg, a0, a1, dense, dg0, dg, o0, b1, b2s, b2,
-        gl, g1, g2s, g2, g3s, g3, g4, g5, send, recv,
+        ga0, ga, gb0, gb, gc0, gc, gd, relay, kept, send, recv,
     ):
         row = lax.axis_index("row")
         p = lax.axis_index("rep")
@@ -74,6 +74,9 @@
                 return [lax.rem(x + d, nx) * 2 + lax.rem(core + e, 2)
                         for d in far_first(nx) + [0] for e in (0, 1) if d or e]
             return [lax.rem(me + d, n) for d in far_first(n)]
+
+        def off(axis, d):
+            return lax.rem(axis[1] + (d + axis[0]), axis[0])
 
         def send_to(axis, t, src, dst, sem, left=None):
             pltpu.make_async_remote_copy(
@@ -139,9 +142,19 @@
         for h, axis in ((0, y_axis), (1, z_axis)):
             wait_bytes(most(f1.at[h], nz), recv.at[2 + h])
             part = dot(node_swap, f1[h].reshape(hpos // ny * cs, width)).astype(BF)
-            f2[h, axis[1]] = part.reshape(cs, nz * half, width)
-            for t in others(axis):
-                send_to(axis, t, f2.at[h, axis[1]], f2.at[h, axis[1]], 4 + h)
+            me = axis[1]
+            f2[h, me] = part.reshape(cs, nz * half, width)
+            for d in (2, -2, 1, -1):
+                sem = {2: M2, -2: P2}.get(d, F2) + h
+                send_to(axis, off(axis, d), f2.at[h, me], f2.at[h, me], sem, F2 + h)
+        for sem, d in ((P2, 2), (M2, -2)):
+            for h, axis in ((0, y_axis), (1, z_axis)):
+                there = off(axis, d)
+                wait_bytes(f2.at[h, there], recv.at[sem + h])
+                whole = f2.at[h, there]
+                send_to(axis, off(axis, -d // 2), whole, whole, F2 + h)
+                part = f2.at[h, there, pl.ds(0 if d > 0 else cs // 2, cs // 2)]
+                send_to(axis, off(axis, -d), part, part, F2 + h)
 
         wait_bytes(most(meta, nrep), recv.at[0])
         codes = meta[0]
@@ -160,7 +173,7 @@
         select = (pos_iota == pos).astype(F32).T.astype(BF)
 
         for h in range(2):
-            wait_bytes(most(f2.at[h], ny), recv.at[4 + h])
+            wait_bytes(f2.at[h, pl.ds(0, 5)], recv.at[F2 + h])
         for c in range(cs):
             here = jnp.concatenate(
                 [f2[0, :, c].reshape(hpos, width), f2[1, :, c].reshape(hpos, width)], axis=0)
@@ -207,82 +220,109 @@
         dg[p] = dg0[...]
         hid_o[...] = (pre * sig).astype(BF)
 
-        contract_rows = (((0,), (0,)), ((), ()))
-        bsum = jnp.sum(dpre, axis=0, keepdims=True)
-        high = bsum.astype(BF).astype(F32)
-        row16 = lax.broadcasted_iota(jnp.int32, (16, width), 0)
-        bias_rows = jnp.zeros((16, width), F32)
-        for at, part in ((0, high), (8, bsum - high)):
-            for s in range(2):
-                bias_rows = jnp.where(row16 == at + s, part[:, s * width:(s + 1) * width], bias_rows)
-        bias_rows = bias_rows.astype(BF)
-        both = jnp.concatenate([own, agg], axis=1)
-        grads = lax.dot_general(both, dpre_b, contract_rows, preferred_element_type=F32)
-        pieces = jnp.concatenate(
-            [grads[w * width:(w + 1) * width, s * width:(s + 1) * width]
-             for w in range(2) for s in range(2)], axis=0)
-        for q in range(nrep):
-            gl[q, 0:wrows, :] = pieces[q * wrows:(q + 1) * wrows].astype(BF)
-            gl[q, wrows:wrows + 16, :] = bias_rows
-        for t in others(rep_axis):
-            send_to(rep_axis, t, gl.at[t], g1.at[p], 13)
-        g1[p] = gl[p]
-
         def summed(buf, n):
             acc = buf[0].astype(F32)
             for q in range(1, n):
                 acc = acc + buf[q].astype(F32)
             return acc
 
+        def two_parts(value):
+            high = value.astype(BF).astype(F32)
+            return jnp.concatenate([high, value - high], axis=0).astype(BF)
+
+        by_half = ((0, y_axis), (1, z_axis))
+        by_other = ((0, z_axis), (1, y_axis))
+        contract_rows = (((0,), (0,)), ((), ()))
+        bsum = jnp.sum(dpre, axis=0, keepdims=True)
+        row8 = lax.broadcasted_iota(jnp.int32, (8, width), 0)
+        bias_rows = two_parts(jnp.where(
+            row8 == 0, bsum[:, :width], jnp.where(row8 == 1, bsum[:, width:], 0.0)))
+        for h, left in ((0, own), (1, agg)):
+            grads = lax.dot_general(left, dpre_b, contract_rows, preferred_element_type=F32)
+            grads = jnp.concatenate([grads[:, :width], grads[:, width:]], axis=0).astype(BF)
+            for q in range(ny):
+                ga0[h, q, 0:grows, :] = grads[q * grows:(q + 1) * grows]
+                if h == 0:
+                    ga0[h, q, grows:, :] = bias_rows
+        rows_in = (grows + 16, grows)
+        for h, axis in by_half:
+            for t in others(axis):
+                send_to(axis, t, ga0.at[h, t, pl.ds(0, rows_in[h])],
+                        ga.at[h, axis[1], pl.ds(0, rows_in[h])], GA + h)
+            ga[h, axis[1]] = ga0[h, axis[1]]
+
+        contract = lax.dot_general(dpre_b, w_self[...], contract_cols, preferred_element_type=F32)
+
         wait_bytes(most(dg, nrep), recv.at[7])
         dall = dg[...].reshape(nodes, width)
-        by_half = ((0, y_axis), (1, z_axis))
+        hc = cs // 2
 
         def back_piece(h, t):
             flat = dense[h, t].reshape(cs * nz * half, nodes)
-            return dot(flat, dall).astype(BF).reshape(cs, nz * half, width)
-
-        def back_send(first, last):
-            for i in range(first, last):
-                for h, axis in by_half:
-                    t = others(axis)[i]
-                    o0[h, t] = back_piece(h, t)
-                    send_to(axis, t, o0.at[h, t], b1.at[h, axis[1]], 8 + h)
-
-        back_send(0, 1)
-
-        wait_bytes(most(g1, nrep), recv.at[13])
-        gsum = summed(g1, nrep)
-        gbias = gsum[wrows:wrows + 8] + gsum[wrows + 8:wrows + 16]
-        for q in range(ny):
-            g2s[q, 0:yrows, :] = gsum[q * yrows:(q + 1) * yrows]
-            g2s[q, yrows:yrows + 8, :] = gbias
-        for t in others(y_axis):
-            send_to(y_axis, t, g2s.at[t], g2.at[y], 14)
-        g2[y] = g2s[y]
-        back_send(1, early)
-
-        wait_bytes(most(g2, ny), recv.at[14])
-        g3s[...] = summed(g2, ny)
-        for t in others(z_axis):
-            send_to(z_axis, t, g3s, g3.at[z], 15)
-        g3[z] = g3s[...]
-        back_send(early, ny - 1)
-        for h, axis in by_half:
-            b1[h, axis[1]] = back_piece(h, axis[1])
-
-        contract = lax.dot_general(dpre_b, w_self[...], contract_cols, preferred_element_type=F32)
-        wait_bytes(most(g3, nz), recv.at[15])
-        gfull = summed(g3, nz) * scale
-        gb_o[...] = jnp.concatenate([gfull[yrows:yrows + 1], gfull[yrows + 1:yrows + 2]], axis=1)
-        g4[y] = gfull[:yrows]
-        for t in others(y_axis):
-            send_to(y_axis, t, g4.at[y], g4.at[y], 16)
+            return dot(flat, dall).reshape(cs, nz * half, width)
+
+        for h, axis in by_half:
+            t = off(axis, 4)
+            o0[h, t] = back_piece(h, t).astype(BF)
+            send_to(axis, off(axis, 2), o0.at[h, t, pl.ds(0, hc)],
+                    relay.at[h, 0, pl.ds(cs, hc)], RP + h, RL + h)
+            send_to(axis, off(axis, -2), o0.at[h, t, pl.ds(hc, hc)],
+                    relay.at[h, 1, pl.ds(cs, hc)], RM + h, RL + h)
+        for h, axis in by_half:
+            for d, sem in ((3, RP), (-3, RM)):
+                t = off(axis, d)
+                o0[h, t] = back_piece(h, t).astype(BF)
+                send_to(axis, off(axis, d // 3), o0.at[h, t],
+                        relay.at[h, 0 if d > 0 else 1, pl.ds(0, cs)], sem + h, RL + h)
+
+        for h, axis in by_half:
+            wait_bytes(ga.at[h, pl.ds(0, ny - 1), pl.ds(0, rows_in[h])], recv.at[GA + h])
+            acc = summed(ga.at[h, :, pl.ds(0, rows_in[h])], ny)
+            gb0[h, 0:grows] = acc[:grows].astype(BF)
+            if h == 0:
+                gb0[h, grows:] = two_parts(acc[grows:grows + 8] + acc[grows + 8:])
+        for h, axis in by_other:
+            for t in others(axis):
+                send_to(axis, t, gb0.at[h, pl.ds(0, rows_in[h])],
+                        gb.at[h, axis[1], pl.ds(0, rows_in[h])], GB + h)
+            gb[h, axis[1]] = gb0[h]
+
+        for h, axis in by_half:
+            for d, slot in ((1, 0), (-1, 1)):
+                t = off(axis, d)
+                o0[h, t] = back_piece(h, t).astype(BF)
+                send_to(axis, t, o0.at[h, t], b1.at[h, slot], B1 + h)
+        for h, axis in by_half:
+            for d, way, sem in ((2, 0, RP), (-2, 1, RM)):
+                t = off(axis, d)
+                made = back_piece(h, t)
+                wait_bytes(relay.at[h, way], recv.at[sem + h])
+                passed = relay[h, way].astype(F32)
+                low, high = made[:hc] + passed[:hc], made[hc:] + passed[hc:cs]
+                if d > 0:
+                    low = low + passed[cs:]
+                else:
+                    high = high + passed[cs:]
+                o0[h, t, 0:hc] = low.astype(BF)
+                o0[h, t, hc:cs] = high.astype(BF)
+                send_to(axis, t, o0.at[h, t], b1.at[h, 2 + way], B1 + h)
+        for h, axis in by_half:
+            kept[h] = back_piece(h, axis[1])
+
+        for h, axis in by_other:
+            wait_bytes(gb.at[h, pl.ds(0, nz - 1), pl.ds(0, rows_in[h])], recv.at[GB + h])
+            acc = summed(gb.at[h, :, pl.ds(0, rows_in[h])], nz)
+            gc0[h * grows:(h + 1) * grows] = acc[:grows].astype(BF)
+            if h == 0:
+                gc0[2 * grows:] = two_parts(acc[grows:grows + 8] + acc[grows + 8:])
+        for t in others(rep_axis):
+            send_to(rep_axis, t, gc0, gc.at[p], GC)
+        gc[p] = gc0[...]
 
         back_swap = node_swap if cs == nz * half else swap_matrix(cs, nz * half)
         for h, axis in ((0, z_axis), (1, y_axis)):
-            wait_bytes(most(b1.at[h], ny), recv.at[8 + h])
-            acc = summed(b1.at[h], ny).reshape(hpos // ny * cs, width).astype(BF)
+            wait_bytes(b1.at[h], recv.at[B1 + h])
+            acc = (kept[h] + summed(b1.at[h], 4)).reshape(hpos // ny * cs, width).astype(BF)
             b2s[h] = dot(back_swap, acc).astype(BF).reshape(nz, half, cs, width)
             for t in others(axis) + [None]:
                 for low in range(half):
@@ -309,25 +349,34 @@
                     def _():
                         send_to(rep_axis, to, mine, into, 10, 18 + b)
 
-        wait_bytes(most(g4, ny), recv.at[16])
-        g5[p] = g4[...].reshape(wrows, width).astype(BF)
-        for t in others(rep_axis):
-            send_to(rep_axis, t, g5.at[p], g5.at[p], 17)
+        wait_bytes(most(gc, nrep), recv.at[GC])
+        acc = summed(gc, nrep) * scale
+        gbias = acc[2 * grows:2 * grows + 8] + acc[2 * grows + 8:]
+        gb_o[...] = jnp.concatenate([gbias[0:1], gbias[1:2]], axis=1)
+        for h, axis in by_half:
+            me = axis[1]
+            gd[h, me] = acc[h * grows:(h + 1) * grows].astype(BF)
+            for t in others(axis):
+                send_to(axis, t, gd.at[h, me], gd.at[h, me], GD + h)
 
         wait_bytes(b2, recv.at[10])
         gf_o[...] = contract + summed(b2, nz).reshape(share, width)
-        wait_bytes(most(g5, nrep), recv.at[17])
-        every = g5[...].reshape(4, width, width).astype(F32)
-        for s in range(2):
-            gs_o[:, s * width:(s + 1) * width] = every[s]
-            gn_o[:, s * width:(s + 1) * width] = every[2 + s]
+        for h, out in ((0, gs_o), (1, gn_o)):
+            wait_bytes(most(gd.at[h], ny), recv.at[GD + h])
+            every = gd[h].reshape(2, width, width).astype(F32)
+            for c in range(2):
+                out[:, c * width:(c + 1) * width] = every[c]
 
         wait_bytes(most(meta, nrep), send.at[0])
         wait_bytes(most(tt, nrep), send.at[1])
         for h in range(2):
             wait_bytes(most(f1.at[h], nz), send.at[2 + h])
-            wait_bytes(most(f2.at[h], nz), send.at[4 + h])
-            wait_bytes(most(b1.at[h], nz), send.at[8 + h])
+            wait_bytes(most(f2.at[h], nz), send.at[F2 + h])
+            wait_bytes(relay.at[h], send.at[RL + h])
+            wait_bytes(b1.at[h], send.at[B1 + h])
+            wait_bytes(ga.at[h, pl.ds(0, ny - 1), pl.ds(0, rows_in[h])], send.at[GA + h])
+            wait_bytes(gb.at[h, pl.ds(0, nz - 1), pl.ds(0, rows_in[h])], send.at[GB + h])
+            wait_bytes(most(gd.at[h], ny), send.at[GD + h])
         wait_bytes(most(a1, nrep), send.at[6])
         wait_bytes(most(dg, nrep), send.at[7])
         wait_bytes(most(b2, nz), send.at[10])
@@ -337,11 +386,7 @@
             @pl.when(node // share != p)
             def _():
                 wait_bytes(b2s.at[0, 0, 0], send.at[18 + b])
-        wait_bytes(most(g1, nrep), send.at[13])
-        wait_bytes(most(g2, ny), send.at[14])
-        wait_bytes(most(g3, nz), send.at[15])
-        wait_bytes(most(g4, ny), send.at[16])
-        wait_bytes(most(g5, nrep), send.at[17])
+        wait_bytes(most(gc, nrep), send.at[GC])
 
     V = pltpu.VMEM
     scratch = [
@@ -360,19 +405,20 @@
         V((share, width), BF),
         V((nrep, share, width), BF),
         V((2, ny, cs, nz * half, width), BF),
-        V((2, ny, cs, nz * half, width), BF),
+        V((2, 4, cs, nz * half, width), BF),
         V((2, nz, half, cs, width), BF),
         V((nz, share // cs, cs, width), BF),
-        V((nrep, wrows + 16, width), BF),
-        V((nrep, wrows + 16, width), BF),
-        V((ny, yrows + 8, width), F32),
-        V((ny, yrows + 8, width), F32),
-        V((yrows + 8, width), F32),
-        V((nz, yrows + 8, width), F32),
-        V((ny, yrows, width), F32),
-        V((nrep, wrows, width), BF),
-        pltpu.SemaphoreType.DMA((22,)),
-        pltpu.SemaphoreType.DMA((18,)),
+        V((2, ny, grows + 16, width), BF),
+        V((2, ny, grows + 16, width), BF),
+        V((2, grows + 16, width), BF),
+        V((2, nz, grows + 16, width), BF),
+        V((2 * grows + 16, width), BF),
+        V((nrep, 2 * grows + 16, width), BF),
+        V((2, ny, grows, width), BF),
+        V((2, 2, cs + cs // 2, nz * half, width), BF),
+        V((2, cs, nz * half, width), F32),
+        pltpu.SemaphoreType.DMA((40,)),
+        pltpu.SemaphoreType.DMA((40,)),
     ]
     outs = (
         jax.ShapeDtypeStruct((share, hid), BF),

time: 70.3 us -> 62.6 us (0.89)
  Pallas kernels: 69.5 us -> 61.8 us
    pallas_call x1, Pallas kernels: 67.7 us -> 60 us  [per_device(): call(features.reshape(nbd, blk, width), edge_tiles, tile_owner.reshape(tp...]
where the time goes in v3:
time: 62.6 us; the launch traced here: 62.4 us
  Pallas kernels  61.8 us (99%)
  between operations  0.64 us (1%)
    pallas_call x1, Pallas kernels, per_device(): call(features.reshape(nbd, blk, width), edge_tiles, tile_owner.reshape(tp...  60 us
    pallas_call x1, Pallas kernels, finish(): pl.pallas_call(kernel, out_shape=tuple((jax.ShapeDtypeStruct(r.shape, r.d...  1.78 us

profile of v3, /device:TPU:1, one launch (start us, length us, event | category | flops | bytes accessed | tf_op | source)
XLA Modules:
  0.0 62.4 jit_solution(417669774703253254)
XLA Ops:
  0.6 60.0 %shard_map.128 = (bf16[64,256]{1,0:T(8,128)(2,1)}, f32[64,128]{1,0:T(8,128)}, f32[128,256]{1,0:T(8,128)}, f32[128,256]{1,0:T(8,128)}, f32[1,256]{1,0:T(1,128)}) custom-call(bf16[4,128,128]{2,1,0:T(8,128)(2,1)} %bitcast.4, bf16[16,128,128]{2,1,0:T(8,128)(2,1)} %tiles.1, s32[16]{0:T(128)} %bitcast.6, s32[16]{0:T(128)} %tblock.1, s32[16]{0:T(128)} %trow.1, ...), custom_call_target="tpu_custom_call" | custom-call | tf_op jit(solution)/shard_map/pallas_call | solution.py:472
  60.6 1.8 %shard_map.129 = (bf16[64,256]{1,0:T(8,128)(2,1)}, f32[64,128]{1,0:T(8,128)}, f32[128,256]{1,0:T(8,128)}, f32[128,256]{1,0:T(8,128)}, f32[1,256]{1,0:T(1,128)}) custom-call(bf16[64,256]{1,0:T(8,128)(2,1)} %get-tuple-element.15.refs_0_, f32[64,128]{1,0:T(8,128)} %get-tuple-element.16.refs_1_, f32[128,256]{1,0:T(8,128)} %get-tuple-element.17.refs_2_, ...), custom_call_target="tpu_custom_call" | custom-call | tf_op jit(solution)/shard_map/pallas_call | solution.py:452

commit v4 on v3

--- a/solution.py
+++ b/solution.py
@@ -33,15 +33,17 @@
     scale = float(nz * ny * nodes) ** -0.5
     assert nz == ny == 8 and hid == 2 * width
     grows = 2 * width // ny
-    F2, P2, M2, B1, RL, RP, RM, GA, GB, GD = range(20, 40, 2)
+    F1N, F1F, F2, F3, B1N, B1F, GA, GB, GD = range(20, 38, 2)
+    RL, F2N, F2F, RLN, RLF = range(40, 60, 4)
     GC = 13
     nx = nrep // 2
 
     def kernel(
-        feat, tiles, owner, tblock, trow, w_self, w_neigh, bias, cot,
+        feat_in, tiles_in, owner, tblock, trow, w_self_in, w_neigh_in, bias_in, cot_in,
         hid_o, gf_o, gs_o, gn_o, gb_o,
-        meta_s, meta, xt, ysend, tt, f1, f2, ttm, fg, a0, a1, dense, dg0, dg, o0, b1, b2s, b2,
-        ga0, ga, gb0, gb, gc0, gc, gd, relay, kept, send, recv,
+        meta_s, meta, xt, ysend, tt, f2, turned, a0, a1, dense0, dense, dg0, dg, o0, b1, b2s, b2,
+        ga0, ga, gb0, gb, gc0, gc, gd, relay3, relay4, kept,
+        feat, tiles, w_self, w_neigh, bias, cot, load, send, recv,
     ):
         row = lax.axis_index("row")
         p = lax.axis_index("rep")
@@ -75,6 +77,11 @@
                         for d in far_first(nx) + [0] for e in (0, 1) if d or e]
             return [lax.rem(me + d, n) for d in far_first(n)]
 
+        def seen(d):
+            return (2 - d) % 8
+
+        near, far = pl.ds(0, 5), pl.ds(5, 3)
+
         def off(axis, d):
             return lax.rem(axis[1] + (d + axis[0]), axis[0])
 
@@ -93,10 +100,31 @@
 
         barrier = pltpu.get_barrier_semaphore()
         count = 0
-        for axis in axes:
-            for t in others(axis):
+        for axis in (z_axis, y_axis, rep_axis):
+            greeted = others(axis) if axis is rep_axis else [off(axis, d) for d in (2, -2, 1, -1)]
+            for t in greeted:
                 pl.semaphore_signal(barrier, inc=1, device_id=axis[2](t), device_id_type=MESH)
                 count += 1
+
+        loads = [
+            pltpu.make_async_copy(src, dst, load.at[i]) for i, (src, dst) in enumerate((
+                (feat_in, feat), (tiles_in, tiles), (w_self_in, w_self),
+                (w_neigh_in, w_neigh), (bias_in, bias), (cot_in, cot)))]
+        for copy in loads:
+            copy.start()
+
+        pl.semaphore_wait(barrier, count)
+
+        loads[0].wait()
+        start = pl.multiple_of(p * cs, cs)
+        by_half = ((0, y_axis), (1, z_axis))
+        by_other = ((0, z_axis), (1, y_axis))
+        for d in (2, -2, 1, -1):
+            for h, axis in by_other:
+                send_to(axis, off(axis, d), feat.at[pl.ds(h * half, half), pl.ds(start, cs), :],
+                        f2.at[h, 2, seen(d)], F1N + h)
+        for h in range(2):
+            f2[h, 2, 2] = feat[pl.ds(h * half, half), pl.ds(start, cs), :]
 
         lane = lax.broadcasted_iota(jnp.int32, (8, tiles_all), 1)
         code = jnp.zeros((8, tiles_all), jnp.int32)
@@ -106,29 +134,20 @@
             own_y = own - own_z * ny
             b = tblock[k]
             low = b - (b // half) * half
-            first = own_y * (2 * nz) + own_z * half + low
-            second = hpos + own_z * (2 * ny) + own_y * half + low
+            rel_z, rel_y = lax.rem(own_z - z + nz + 2, nz), lax.rem(own_y - y + ny + 2, ny)
+            first = rel_y * (2 * nz) + rel_z * half + low
+            second = hpos + rel_z * (2 * ny) + rel_y * half + low
             where_to = jnp.where(b < half, first, second) + trow[k] * npos
             code = jnp.where(lane == p * tpd + k, where_to, code)
         meta_s[...] = code
-
-        pl.semaphore_wait(barrier, count)
-
-        start = pl.multiple_of(p * cs, cs)
-        f1[0, z] = feat[pl.ds(0, half), pl.ds(start, cs), :]
-        f1[1, y] = feat[pl.ds(half, half), pl.ds(start, cs), :]
-        for h, axis in ((0, z_axis), (1, y_axis)):
-            for t in others(axis):
-                send_to(axis, t, feat.at[pl.ds(h * half, half), pl.ds(start, cs), :],
-                        f1.at[h, axis[1]], 2 + h)
         for t in others(rep_axis):
             send_to(rep_axis, t, meta_s, meta.at[p], 0)
         meta[p] = code
 
+        loads[1].wait()
         for k in range(tpd):
             xt[k] = tiles[k].T
         tile_swap = swap_matrix(tpd, cs)
-        node_swap = swap_matrix(nz * half, cs)
 
         def columns_of(t):
             part = xt[:, pl.ds(pl.multiple_of(t * cs, cs), cs), :].reshape(tpd * cs, blk)
@@ -139,22 +158,36 @@
             send_to(rep_axis, t, ysend.at[t], tt.at[p], 1)
         tt[p] = columns_of(p)
 
-        for h, axis in ((0, y_axis), (1, z_axis)):
-            wait_bytes(most(f1.at[h], nz), recv.at[2 + h])
-            part = dot(node_swap, f1[h].reshape(hpos // ny * cs, width)).astype(BF)
-            me = axis[1]
-            f2[h, me] = part.reshape(cs, nz * half, width)
+        for batch, sem1, sem2, size in ((near, F1N, F2N, 4), (far, F1F, F2F, 3)):
+            for h, axis in by_other:
+                wait_bytes(f2.at[h, 2, pl.ds(0, size)], recv.at[sem1 + h])
+                if sem1 != F1N:
+                    continue
+                for d in (2, -2):
+                    got = f2.at[h, 2, 2 + d]
+                    send_to(axis, off(axis, -d // 2), got, f2.at[h, 2, 5 if d > 0 else 7],
+                            F1F + h, F1N + h)
+                    part = pl.ds(half // 2 if d > 0 else 0, half // 2)
+                    send_to(axis, off(axis, -d), got.at[part], f2.at[h, 2, 6, part],
+                            F1F + h, F1N + h)
             for d in (2, -2, 1, -1):
-                sem = {2: M2, -2: P2}.get(d, F2) + h
-                send_to(axis, off(axis, d), f2.at[h, me], f2.at[h, me], sem, F2 + h)
-        for sem, d in ((P2, 2), (M2, -2)):
-            for h, axis in ((0, y_axis), (1, z_axis)):
-                there = off(axis, d)
-                wait_bytes(f2.at[h, there], recv.at[sem + h])
-                whole = f2.at[h, there]
-                send_to(axis, off(axis, -d // 2), whole, whole, F2 + h)
-                part = f2.at[h, there, pl.ds(0 if d > 0 else cs // 2, cs // 2)]
-                send_to(axis, off(axis, -d), part, part, F2 + h)
+                for h, axis in by_half:
+                    sem = sem2 + 2 * h + (d < 0) if abs(d) == 2 else F2 + h
+                    send_to(axis, off(axis, d), f2.at[h, 2, batch], f2.at[h, seen(d), batch],
+                            sem, F2 + h)
+
+        def pass_on(batch, sem2, parts):
+            for d in (2, -2):
+                for h, axis in by_half:
+                    there = (2 + d) % 8
+                    wait_bytes(f2.at[h, there, batch], recv.at[sem2 + 2 * h + (d > 0)])
+                    send_to(axis, off(axis, -d // 2), f2.at[h, there, batch],
+                            f2.at[h, 5 if d > 0 else 7, batch], F3 + h, F2 + h)
+                    part = parts[d > 0]
+                    send_to(axis, off(axis, -d), f2.at[h, there, part], f2.at[h, 6, part],
+                            F3 + h, F2 + h)
+
+        pass_on(near, F2N, (pl.ds(0, 3), pl.ds(3, 2)))
 
         wait_bytes(most(meta, nrep), recv.at[0])
         codes = meta[0]
@@ -164,26 +197,7 @@
         rows_of = codes // npos
         pos = codes - rows_of * npos
         wait_bytes(most(tt, nrep), recv.at[1])
-        for c in range(cs):
-            turned = tt[:, c].reshape(tiles_all, blk).T
-            for n in range(nbd):
-                ttm[n * blk:(n + 1) * blk, c * tiles_all:(c + 1) * tiles_all] = jnp.where(
-                    rows_of == n, turned, jnp.zeros_like(turned))
         pos_iota = lax.broadcasted_iota(jnp.int32, (npos, tiles_all), 0)
-        select = (pos_iota == pos).astype(F32).T.astype(BF)
-
-        for h in range(2):
-            wait_bytes(f2.at[h, pl.ds(0, 5)], recv.at[F2 + h])
-        for c in range(cs):
-            here = jnp.concatenate(
-                [f2[0, :, c].reshape(hpos, width), f2[1, :, c].reshape(hpos, width)], axis=0)
-            fg[c * tiles_all:(c + 1) * tiles_all, :] = dot(select, here).astype(BF)
-        partial = dot(ttm[...], fg[...]).astype(BF).reshape(nrep, share, width)
-        a0[...] = partial
-        for t in others(rep_axis):
-            send_to(rep_axis, t, a0.at[t], a1.at[p], 6)
-        a1[p] = a0[p]
-
         spread = jnp.concatenate(
             [(pos_iota + n * npos == codes).astype(F32).astype(BF) for n in range(nbd)], axis=0)
         for c in range(cs):
@@ -191,9 +205,33 @@
             for n in range(nbd):
                 for h in range(2):
                     at = n * npos + h * hpos
-                    dense[h, :, c, :, n * blk:(n + 1) * blk] = placed[at:at + hpos].reshape(
+                    dense0[h, :, c, :, n * blk:(n + 1) * blk] = placed[at:at + hpos].reshape(
                         ny, nz * half, blk)
 
+        pass_on(far, F2F, (pl.ds(5, 1), pl.ds(6, 2)))
+        chunk = nz * half * cs
+        node_swap = swap_matrix(cs, nz * half)
+        for h in range(2):
+            for t in range(ny):
+                piece = dot(node_swap, dense0[h, t].reshape(chunk, nodes)).astype(BF)
+                dense[h, t] = piece
+                at = (h * ny + t) * chunk
+                turned[:, at:at + chunk] = piece.T
+
+        for part, size, sem in ((slice(0, 5), 2, F2), (slice(5, 8), 3, F3)):
+            for h in range(2):
+                wait_bytes(f2.at[h, pl.ds(8 - size, size)], recv.at[sem + h])
+                n = (part.stop - part.start) * chunk
+                at = (h * ny + part.start) * chunk
+                made = dot(turned[:, at:at + n], f2[h, part].reshape(n, width))
+                partial = made if h == 0 and sem == F2 else partial + made
+        a0[...] = partial.astype(BF).reshape(nrep, share, width)
+        for t in others(rep_axis):
+            send_to(rep_axis, t, a0.at[t], a1.at[p], 6)
+        a1[p] = a0[p]
+
+        for copy in loads[2:]:
+            copy.wait()
         per_block = blk // share if share < blk else 1
         if share < blk:
             which = p // per_block
@@ -230,8 +268,6 @@
             high = value.astype(BF).astype(F32)
             return jnp.concatenate([high, value - high], axis=0).astype(BF)
 
-        by_half = ((0, y_axis), (1, z_axis))
-        by_other = ((0, z_axis), (1, y_axis))
         contract_rows = (((0,), (0,)), ((), ()))
         bsum = jnp.sum(dpre, axis=0, keepdims=True)
         row8 = lax.broadcasted_iota(jnp.int32, (8, width), 0)
@@ -255,25 +291,41 @@
 
         wait_bytes(most(dg, nrep), recv.at[7])
         dall = dg[...].reshape(nodes, width)
-        hc = cs // 2
 
         def back_piece(h, t):
-            flat = dense[h, t].reshape(cs * nz * half, nodes)
-            return dot(flat, dall).reshape(cs, nz * half, width)
-
-        for h, axis in by_half:
-            t = off(axis, 4)
-            o0[h, t] = back_piece(h, t).astype(BF)
-            send_to(axis, off(axis, 2), o0.at[h, t, pl.ds(0, hc)],
-                    relay.at[h, 0, pl.ds(cs, hc)], RP + h, RL + h)
-            send_to(axis, off(axis, -2), o0.at[h, t, pl.ds(hc, hc)],
-                    relay.at[h, 1, pl.ds(cs, hc)], RM + h, RL + h)
-        for h, axis in by_half:
-            for d, sem in ((3, RP), (-3, RM)):
-                t = off(axis, d)
-                o0[h, t] = back_piece(h, t).astype(BF)
-                send_to(axis, off(axis, d // 3), o0.at[h, t],
-                        relay.at[h, 0 if d > 0 else 1, pl.ds(0, cs)], sem + h, RL + h)
+            return dot(dense[h, t], dall).reshape(nz, half * cs, width)
+
+        def relay_four(sem, plus, minus):
+            for h, axis in by_half:
+                for d, part in ((2, plus), (-2, minus)):
+                    send_to(axis, off(axis, d), o0.at[h, 6, part], relay4.at[h, part],
+                            sem + 2 * h + (d < 0), RL + 2 + h)
+
+        def relay_three(batch, sem):
+            for h, axis in by_half:
+                for d, t in ((1, 5), (-1, 7)):
+                    send_to(axis, off(axis, d), o0.at[h, t, batch],
+                            relay3.at[h, int(d < 0), batch], sem + 2 * h + (d < 0), RL + h)
+
+        def next_out(batch, sem):
+            for h, axis in by_half:
+                for d, slot in ((1, 0), (-1, 1)):
+                    send_to(axis, off(axis, d), o0.at[h, 2 + d, batch], b1.at[h, slot, batch],
+                            sem + h, B1N + h)
+
+        def make(*places):
+            for t in places:
+                for h in range(2):
+                    o0[h, t] = back_piece(h, t).astype(BF)
+
+        make(6)
+        relay_four(RLF, pl.ds(5, 1), pl.ds(6, 2))
+        make(5, 7)
+        relay_three(far, RLF)
+        relay_four(RLN, pl.ds(0, 3), pl.ds(3, 2))
+        relay_three(near, RLN)
+        make(1, 3)
+        next_out(far, B1F)
 
         for h, axis in by_half:
             wait_bytes(ga.at[h, pl.ds(0, ny - 1), pl.ds(0, rows_in[h])], recv.at[GA + h])
@@ -287,27 +339,29 @@
                         gb.at[h, axis[1], pl.ds(0, rows_in[h])], GB + h)
             gb[h, axis[1]] = gb0[h]
 
-        for h, axis in by_half:
-            for d, slot in ((1, 0), (-1, 1)):
-                t = off(axis, d)
-                o0[h, t] = back_piece(h, t).astype(BF)
-                send_to(axis, t, o0.at[h, t], b1.at[h, slot], B1 + h)
-        for h, axis in by_half:
-            for d, way, sem in ((2, 0, RP), (-2, 1, RM)):
-                t = off(axis, d)
-                made = back_piece(h, t)
-                wait_bytes(relay.at[h, way], recv.at[sem + h])
-                passed = relay[h, way].astype(F32)
-                low, high = made[:hc] + passed[:hc], made[hc:] + passed[hc:cs]
-                if d > 0:
-                    low = low + passed[cs:]
-                else:
-                    high = high + passed[cs:]
-                o0[h, t, 0:hc] = low.astype(BF)
-                o0[h, t, hc:cs] = high.astype(BF)
-                send_to(axis, t, o0.at[h, t], b1.at[h, 2 + way], B1 + h)
-        for h, axis in by_half:
-            kept[h] = back_piece(h, axis[1])
+        next_out(near, B1N)
+        for h in range(2):
+            kept[h, 0] = back_piece(h, 2)
+            kept[h, 1] = back_piece(h, 4)
+            kept[h, 2] = back_piece(h, 0)
+
+        for lo, hi, sem, sem_out, cuts in ((5, 8, RLF, B1F, (6, 4, 5)), (0, 5, RLN, B1N, (3, 8, 7))):
+            cut = cuts[0]
+            for h, axis in by_half:
+                for way, d in ((0, 2), (1, -2)):
+                    wait_bytes(relay3.at[h, way, pl.ds(0, cuts[1 + way])],
+                               recv.at[sem + 2 * h + way])
+                    made = kept[h, 1 + way, lo:hi] + relay3[h, way, lo:hi].astype(F32)
+                    first, second = made[:cut - lo], made[cut - lo:]
+                    if way == 0:
+                        first = first + relay4[h, lo:cut].astype(F32)
+                    else:
+                        second = second + relay4[h, cut:hi].astype(F32)
+                    t = 2 + d
+                    o0[h, t, lo:cut] = first.astype(BF)
+                    o0[h, t, cut:hi] = second.astype(BF)
+                    send_to(axis, off(axis, d), o0.at[h, t, pl.ds(lo, hi - lo)],
+                            b1.at[h, 2 + way, pl.ds(lo, hi - lo)], sem_out + h, B1N + h)
 
         for h, axis in by_other:
             wait_bytes(gb.at[h, pl.ds(0, nz - 1), pl.ds(0, rows_in[h])], recv.at[GB + h])
@@ -319,35 +373,36 @@
             send_to(rep_axis, t, gc0, gc.at[p], GC)
         gc[p] = gc0[...]
 
-        back_swap = node_swap if cs == nz * half else swap_matrix(cs, nz * half)
-        for h, axis in ((0, z_axis), (1, y_axis)):
-            wait_bytes(b1.at[h], recv.at[B1 + h])
-            acc = (kept[h] + summed(b1.at[h], 4)).reshape(hpos // ny * cs, width).astype(BF)
-            b2s[h] = dot(back_swap, acc).astype(BF).reshape(nz, half, cs, width)
-            for t in others(axis) + [None]:
-                for low in range(half):
-                    b = h * half + low
-                    node = b * blk + p * cs
-                    to = node // share
-                    slot = (node - to * share) // cs
-                    into = b2.at[axis[1], slot]
-                    if t is not None:
-                        place = (t * ny + y, to) if h == 0 else (z * ny + t, to)
-                        pltpu.make_async_remote_copy(
-                            src_ref=b2s.at[h, t, low], dst_ref=into, send_sem=send.at[10],
-                            recv_sem=recv.at[10], device_id=place, device_id_type=MESH,
-                        ).start()
-                        continue
-
-                    mine = b2s.at[h, axis[1], low]
-
-                    @pl.when(to == p)
-                    def _():
-                        pltpu.make_async_copy(mine, into, recv.at[10]).start()
-
-                    @pl.when(to != p)
-                    def _():
-                        send_to(rep_axis, to, mine, into, 10, 18 + b)
+        for lo, hi, sem, order in ((5, 8, B1F, (4, 3, -3)), (0, 5, B1N, (2, -2, 1, -1, 0))):
+            for h, axis in by_other:
+                wait_bytes(b1.at[h, :, pl.ds(lo, hi - lo)], recv.at[sem + h])
+                acc = kept[h, 0, lo:hi]
+                for q in range(4):
+                    acc = acc + b1[h, q, lo:hi].astype(F32)
+                b2s[h, lo:hi] = acc.astype(BF).reshape(hi - lo, half, cs, width)
+                for d in order:
+                    for low in range(half):
+                        b = h * half + low
+                        node = b * blk + p * cs
+                        to = node // share
+                        into = b2.at[seen(d), (node - to * share) // cs]
+                        mine = b2s.at[h, (2 + d) % 8, low]
+                        if d != 0:
+                            t = off(axis, d)
+                            place = (t * ny + y, to) if h == 0 else (z * ny + t, to)
+                            pltpu.make_async_remote_copy(
+                                src_ref=mine, dst_ref=into, send_sem=send.at[10],
+                                recv_sem=recv.at[10], device_id=place, device_id_type=MESH,
+                            ).start()
+                            continue
+
+                        @pl.when(to == p)
+                        def _():
+                            pltpu.make_async_copy(mine, into, recv.at[10]).start()
+
+                        @pl.when(to != p)
+                        def _():
+                            send_to(rep_axis, to, mine, into, 10, 14 + b)
 
         wait_bytes(most(gc, nrep), recv.at[GC])
         acc = summed(gc, nrep) * scale
@@ -370,10 +425,11 @@
         wait_bytes(most(meta, nrep), send.at[0])
         wait_bytes(most(tt, nrep), send.at[1])
         for h in range(2):
-            wait_bytes(most(f1.at[h], nz), send.at[2 + h])
-            wait_bytes(most(f2.at[h], nz), send.at[F2 + h])
-            wait_bytes(relay.at[h], send.at[RL + h])
-            wait_bytes(b1.at[h], send.at[B1 + h])
+            wait_bytes(f2.at[h, 2, pl.ds(0, 7)], send.at[F1N + h])
+            wait_bytes(f2.at[h, pl.ds(0, 7)], send.at[F2 + h])
+            wait_bytes(relay3.at[h], send.at[RL + h])
+            wait_bytes(relay4.at[h], send.at[RL + 2 + h])
+            wait_bytes(b1.at[h], send.at[B1N + h])
             wait_bytes(ga.at[h, pl.ds(0, ny - 1), pl.ds(0, rows_in[h])], send.at[GA + h])
             wait_bytes(gb.at[h, pl.ds(0, nz - 1), pl.ds(0, rows_in[h])], send.at[GB + h])
             wait_bytes(most(gd.at[h], ny), send.at[GD + h])
@@ -385,7 +441,7 @@
 
             @pl.when(node // share != p)
             def _():
-                wait_bytes(b2s.at[0, 0, 0], send.at[18 + b])
+                wait_bytes(b2s.at[0, 0, 0], send.at[14 + b])
         wait_bytes(most(gc, nrep), send.at[GC])
 
     V = pltpu.VMEM
@@ -395,17 +451,16 @@
         V((tpd, blk, blk), BF),
         V((nrep, cs, tpd, blk), BF),
         V((nrep, cs, tpd, blk), BF),
-        V((2, nz, half, cs, width), BF),
-        V((2, ny, cs, nz * half, width), BF),
-        V((nodes, cs * tiles_all), BF),
-        V((cs * tiles_all, width), BF),
+        V((2, ny, nz, half, cs, width), BF),
+        V((nodes, npos * cs), BF),
         V((nrep, share, width), BF),
         V((nrep, share, width), BF),
         V((2, ny, cs, nz * half, nodes), BF),
+        V((2, ny, nz * half * cs, nodes), BF),
         V((share, width), BF),
         V((nrep, share, width), BF),
-        V((2, ny, cs, nz * half, width), BF),
-        V((2, 4, cs, nz * half, width), BF),
+        V((2, ny, nz, half * cs, width), BF),
+        V((2, 4, nz, half * cs, width), BF),
         V((2, nz, half, cs, width), BF),
         V((nz, share // cs, cs, width), BF),
         V((2, ny, grows + 16, width), BF),
@@ -415,10 +470,18 @@
         V((2 * grows + 16, width), BF),
         V((nrep, 2 * grows + 16, width), BF),
         V((2, ny, grows, width), BF),
-        V((2, 2, cs + cs // 2, nz * half, width), BF),
-        V((2, cs, nz * half, width), F32),
-        pltpu.SemaphoreType.DMA((40,)),
-        pltpu.SemaphoreType.DMA((40,)),
+        V((2, 2, nz, half * cs, width), BF),
+        V((2, nz, half * cs, width), BF),
+        V((2, 3, nz, half * cs, width), F32),
+        V((nbd, blk, width), BF),
+        V((tpd, blk, blk), BF),
+        V((width, hid), BF),
+        V((width, hid), BF),
+        V((1, hid), F32),
+        V((share, hid), BF),
+        pltpu.SemaphoreType.DMA((6,)),
+        pltpu.SemaphoreType.DMA((60,)),
+        pltpu.SemaphoreType.DMA((60,)),
     ]
     outs = (
         jax.ShapeDtypeStruct((share, hid), BF),
@@ -428,10 +491,11 @@
         jax.ShapeDtypeStruct((1, hid), F32),
     )
     vmem, smem = pl.BlockSpec(memory_space=pltpu.VMEM), pl.BlockSpec(memory_space=pltpu.SMEM)
+    there = pl.BlockSpec(memory_space=pl.ANY)
     return pl.pallas_call(
         kernel,
         out_shape=outs,
-        in_specs=[vmem, vmem, smem, smem, smem, vmem, vmem, vmem, vmem],
+        in_specs=[there, there, smem, smem, smem, there, there, there, there],
         out_specs=tuple([vmem] * 5),
         scratch_shapes=scratch,
         compiler_params=pltpu.CompilerParams(

time: 62.6 us -> 61.6 us (0.984)
  Pallas kernels: 61.8 us -> 60.8 us
    pallas_call x1, Pallas kernels: 60 us -> 59.1 us  [per_device(): call(features.reshape(nbd, blk, width), edge_tiles, tile_owner.reshape(tp...]
where the time goes in v4:
time: 61.6 us; the launch traced here: 61.5 us
  Pallas kernels  60.8 us (99%)
  between operations  0.64 us (1%)
    pallas_call x1, Pallas kernels, per_device(): call(features.reshape(nbd, blk, width), edge_tiles, tile_owner.reshape(tp...  59.1 us
    pallas_call x1, Pallas kernels, finish(): pl.pallas_call(kernel, out_shape=tuple((jax.ShapeDtypeStruct(r.shape, r.d...  1.78 us

profile of v4, /device:TPU:1, one launch (start us, length us, event | category | flops | bytes accessed | tf_op | source)
XLA Modules:
  0.0 61.5 jit_solution(10041304076802664119)
XLA Ops:
  0.6 59.1 %shard_map.128 = (bf16[64,256]{1,0:T(8,128)(2,1)}, f32[64,128]{1,0:T(8,128)}, f32[128,256]{1,0:T(8,128)}, f32[128,256]{1,0:T(8,128)}, f32[1,256]{1,0:T(1,128)}) custom-call(bf16[4,128,128]{2,1,0:T(8,128)(2,1)} %bitcast.4, bf16[16,128,128]{2,1,0:T(8,128)(2,1)} %tiles_in.1, s32[16]{0:T(128)} %bitcast.6, s32[16]{0:T(128)} %tblock.1, s32[16]{0:T(128)} %trow.1, ...), custom_call_target="tpu_custom_call" | custom-call | tf_op jit(solution)/shard_map/pallas_call | solution.py:536
  59.7 1.8 %shard_map.129 = (bf16[64,256]{1,0:T(8,128)(2,1)}, f32[64,128]{1,0:T(8,128)}, f32[128,256]{1,0:T(8,128)}, f32[128,256]{1,0:T(8,128)}, f32[1,256]{1,0:T(1,128)}) custom-call(bf16[64,256]{1,0:T(8,128)(2,1)} %get-tuple-element.15.refs_0_, f32[64,128]{1,0:T(8,128)} %get-tuple-element.16.refs_1_, f32[128,256]{1,0:T(8,128)} %get-tuple-element.17.refs_2_, ...), custom_call_target="tpu_custom_call" | custom-call | tf_op jit(solution)/shard_map/pallas_call | solution.py:516

commit v5 on v4

--- a/solution.py
+++ b/solution.py
@@ -188,6 +188,7 @@
                             F3 + h, F2 + h)
 
         pass_on(near, F2N, (pl.ds(0, 3), pl.ds(3, 2)))
+        pass_on(far, F2F, (pl.ds(5, 1), pl.ds(6, 2)))
 
         wait_bytes(most(meta, nrep), recv.at[0])
         codes = meta[0]
@@ -208,7 +209,6 @@
                     dense0[h, :, c, :, n * blk:(n + 1) * blk] = placed[at:at + hpos].reshape(
                         ny, nz * half, blk)
 
-        pass_on(far, F2F, (pl.ds(5, 1), pl.ds(6, 2)))
         chunk = nz * half * cs
         node_swap = swap_matrix(cs, nz * half)
         for h in range(2):

time: 61.6 us -> 62.1 us (level)
  no operation moved by 1% of the time
where the time goes in v5:
time: 62.1 us; the launch traced here: 62 us
  Pallas kernels  61.4 us (99%)
  between operations  0.64 us (1%)
    pallas_call x1, Pallas kernels, per_device(): call(features.reshape(nbd, blk, width), edge_tiles, tile_owner.reshape(tp...  59.6 us
    pallas_call x1, Pallas kernels, finish(): pl.pallas_call(kernel, out_shape=tuple((jax.ShapeDtypeStruct(r.shape, r.d...  1.78 us

profile of v5, /device:TPU:1, one launch (start us, length us, event | category | flops | bytes accessed | tf_op | source)
XLA Modules:
  0.0 62.0 jit_solution(4706984074417552391)
XLA Ops:
  0.6 59.6 %shard_map.128 = (bf16[64,256]{1,0:T(8,128)(2,1)}, f32[64,128]{1,0:T(8,128)}, f32[128,256]{1,0:T(8,128)}, f32[128,256]{1,0:T(8,128)}, f32[1,256]{1,0:T(1,128)}) custom-call(bf16[4,128,128]{2,1,0:T(8,128)(2,1)} %bitcast.4, bf16[16,128,128]{2,1,0:T(8,128)(2,1)} %tiles_in.1, s32[16]{0:T(128)} %bitcast.6, s32[16]{0:T(128)} %tblock.1, s32[16]{0:T(128)} %trow.1, ...), custom_call_target="tpu_custom_call" | custom-call | tf_op jit(solution)/shard_map/pallas_call | solution.py:536
  60.2 1.8 %shard_map.129 = (bf16[64,256]{1,0:T(8,128)(2,1)}, f32[64,128]{1,0:T(8,128)}, f32[128,256]{1,0:T(8,128)}, f32[128,256]{1,0:T(8,128)}, f32[1,256]{1,0:T(1,128)}) custom-call(bf16[64,256]{1,0:T(8,128)(2,1)} %get-tuple-element.15.refs_0_, f32[64,128]{1,0:T(8,128)} %get-tuple-element.16.refs_1_, f32[128,256]{1,0:T(8,128)} %get-tuple-element.17.refs_2_, ...), custom_call_target="tpu_custom_call" | custom-call | tf_op jit(solution)/shard_map/pallas_call | solution.py:516
